TPU v7x, 32 devices: a whole 2x2x4 slice. The times are simulated.
32 devices in a mesh: traj: 16 (over z, x, core), lat: 2 (over y).
Axes of the slice: x: 2, y: 2, z: 4, core: 2. Of those that a mesh axis runs over, the one named last changes fastest.
Arguments:
- ensemble: float32 [16, 56, 192, 384], P('traj', None, 'lat'), may hold values from -4 to 4
- counts: int32 [16], P('traj'), may hold values from 0 to 4, as said below
- mixing: bfloat16 [56, 56], replicated, may hold values from -0.75 to 0.75
- weights: float32 [192], P('lat'), may hold values from 0.5 to 1.5
- legendre: bfloat16 [128, 192, 128], P('lat'), may hold values from -0.5 to 0.5
- to_modes: float32 [56, 56], replicated, may hold values from -0.75 to 0.75
- from_modes: float32 [56, 56], replicated, may hold values from -0.75 to 0.75
- mode_rates: float32 [56], replicated, may hold values from 0.1 to 10
Outputs:
- advanced: float32 [16, 56, 192, 384], P('traj', None, 'lat')
Inputs may be any that keep to these rules, and one draw needn't show every extreme that they name: The counts of all members sum to 16, and some member has exactly 4.
All inputs are finite; a program needn't handle non-finite values.
Results may differ from a plain program's by a relative error of at most 0.015.
Values may be sent and summed in bfloat16 or wider, within the bound.
A program may use at most 64 MiB of HBM per device.

v0:
```python
import math

import jax
import jax.numpy as jnp
from jax import lax
from jax.experimental import pallas as pl
from jax.experimental.pallas import tpu as pltpu
from jax.sharding import PartitionSpec as P

time_step = 0.3
cubic_rate = 0.1


def clone_sources(counts):
    living = (counts > 0).astype(jnp.int32)
    surplus_end = jnp.cumsum(jnp.maximum(counts - 1, 0), dtype=jnp.int32)
    killed_rank = jnp.cumsum(1 - living, dtype=jnp.int32) - (1 - living)
    pulled = jnp.sum(
        (surplus_end[None, :] <= killed_rank[:, None]).astype(jnp.int32), axis=1, dtype=jnp.int32
    )
    members = jnp.arange(counts.shape[0], dtype=jnp.int32)
    return jnp.where(living > 0, members, pulled)


def fourier_tables(wavenumber, component, longitudes):
    positions = jnp.arange(longitudes, dtype=jnp.int32)
    product_index = positions[:, None] * wavenumber[None, :] % longitudes
    angles = 2.0 * math.pi / longitudes * product_index.astype(jnp.float32)
    signed = jnp.where(component[None, :] == 0, jnp.cos(angles), -jnp.sin(angles))
    factor = jnp.where(wavenumber == 0, 1.0, 2.0).astype(jnp.float32)
    return (signed.astype(jnp.bfloat16), (factor[None, :] * signed).T.astype(jnp.bfloat16))


def mode_divisor(mode_rates, degree_count):
    degrees = jnp.arange(degree_count, dtype=jnp.float32)
    degree_ratio = degrees * (degrees + 1.0) / (degree_count * (degree_count + 1.0))
    return 1.0 + mode_rates[:, None] * degree_ratio[None, :]


def grid_section(state_grid, mixing, lat_scale, forward):
    level_count, row_count, col_count = state_grid.shape
    rounded = state_grid.astype(jnp.bfloat16)
    mixing_term = jnp.dot(
        mixing,
        rounded.reshape(level_count, row_count * col_count),
        preferred_element_type=jnp.float32,
    ).reshape(level_count, row_count, col_count)
    tendency = state_grid + time_step * (
        mixing_term - cubic_rate * state_grid * state_grid * state_grid
    )
    grid_rounded = tendency.astype(jnp.bfloat16).reshape(level_count * row_count, col_count)
    fourier_sums = jnp.dot(grid_rounded, forward, preferred_element_type=jnp.float32)
    fourier_sums = fourier_sums.reshape(level_count, row_count, forward.shape[1])
    return (fourier_sums * lat_scale[None, :, None]).astype(jnp.bfloat16)


def implicit_solve(spectral, to_modes, from_modes, divisor):
    modal = (
        jnp.einsum("kl,pmln->pmkn", to_modes, spectral, precision=lax.Precision.HIGHEST)
        / divisor[None, None]
    )
    return jnp.einsum("lk,pmkn->pmln", from_modes, modal, precision=lax.Precision.HIGHEST).astype(
        jnp.bfloat16
    )


def spread_mixing(mixing):
    return jnp.kron(mixing, jnp.eye(8, dtype=mixing.dtype))


def to_coefficients(values, mixer, scale, forward):
    level_count, rows, longitudes = values.shape
    flat = values.reshape(level_count * rows, longitudes)
    mixed = jnp.dot(mixer, flat.astype(jnp.bfloat16), preferred_element_type=jnp.float32)
    tendency = flat + time_step * (mixed - cubic_rate * flat * flat * flat)
    sums = jnp.dot(tendency.astype(jnp.bfloat16), forward, preferred_element_type=jnp.float32)
    return sums.reshape(level_count, rows, forward.shape[1]) * scale[None, :, :1]


def from_bands(bands, backward):
    parts, level_count, rows, width = bands.shape
    total = None
    for part in range(parts):
        term = jnp.dot(
            bands[part].astype(jnp.bfloat16).reshape(level_count * rows, width),
            backward[part * width : (part + 1) * width, :],
            preferred_element_type=jnp.float32,
        )
        total = term if total is None else total + term
    return total.reshape(level_count, rows, backward.shape[1])


def split_columns(pieces, out_ref):
    whole = jnp.concatenate(pieces, axis=1)
    width = out_ref.shape[3]
    for part in range(out_ref.shape[0]):
        out_ref[part] = whole[:, :, part * width : (part + 1) * width].astype(jnp.bfloat16)


def first_kernel(grid_ref, mixer_ref, scale_ref, forward_ref, out_ref):
    pieces = []
    for low in range(0, grid_ref.shape[1], 8):
        values = grid_ref[:, low : low + 8, :]
        scale = scale_ref[low : low + 8, :]
        pieces.append(to_coefficients(values, mixer_ref[...], scale, forward_ref[...]))
    split_columns(pieces, out_ref)


def middle_kernel(bands_ref, backward_ref, mixer_ref, scale_ref, forward_ref, out_ref):
    whole = from_bands(bands_ref[...], backward_ref[...])
    pieces = []
    for low in range(0, whole.shape[1], 8):
        scale = scale_ref[low : low + 8, :]
        values = whole[:, low : low + 8, :]
        pieces.append(to_coefficients(values, mixer_ref[...], scale, forward_ref[...]))
    split_columns(pieces, out_ref)


def last_kernel(bands_ref, backward_ref, out_ref):
    out_ref[...] = from_bands(bands_ref[...], backward_ref[...])


def fixed(array):
    return pl.BlockSpec(array.shape, lambda step: (0,) * array.ndim)


def by_rows(shape, axis, block):
    sizes = tuple(block if at == axis else size for at, size in enumerate(shape))
    return pl.BlockSpec(sizes, lambda step: tuple(step if at == axis else 0 for at in range(len(shape))))


def row_call(kernel, operands, row_axes, out_shape, out_axis, out_type, block):
    rows = out_shape[out_axis]
    specs = [
        fixed(op) if axis is None else by_rows(op.shape, axis, block)
        for op, axis in zip(operands, row_axes)
    ]
    return pl.pallas_call(
        kernel,
        grid=(rows // block,),
        in_specs=specs,
        out_specs=by_rows(out_shape, out_axis, block),
        out_shape=jax.ShapeDtypeStruct(out_shape, out_type),
        compiler_params=pltpu.CompilerParams(vmem_limit_bytes=40 * 1024 * 1024),
    )(*operands)


def local(ensemble, counts, mixing, weights, legendre, to_modes, from_modes, mode_rates):
    traj_count = lax.axis_size("traj")
    lat_count = lax.axis_size("lat")
    local_waves = legendre.shape[0]
    degree_count = legendre.shape[2]
    total_waves = local_waves * lat_count
    longitudes = ensemble.shape[3]
    columns = jnp.arange(2 * total_waves, dtype=jnp.int32)
    within = columns % (2 * local_waves)
    wavenumber = columns // (2 * local_waves) * local_waves + within % local_waves
    component = within // local_waves
    forward, backward = fourier_tables(wavenumber, component, longitudes)
    lat_scale = weights / longitudes
    divisor = mode_divisor(mode_rates, degree_count)
    sources = clone_sources(lax.all_gather(counts, "traj", axis=0, tiled=True))

    def to_spectral(received):
        split_parts = received.reshape(received.shape[0], received.shape[1], 2, local_waves)
        return jnp.einsum(
            "ljpm,mjn->pmln", split_parts, legendre, preferred_element_type=jnp.float32
        )

    def to_grid(received):
        flat_rows = received.reshape(received.shape[0] * received.shape[1], received.shape[2])
        result_grid = jnp.dot(flat_rows, backward, preferred_element_type=jnp.float32)
        return result_grid.reshape(received.shape[0], received.shape[1], longitudes)

    def to_implicit(coefficients):
        spectral = to_spectral(
            lax.all_to_all(coefficients, "lat", split_axis=2, concat_axis=1, tiled=True)
        )
        return implicit_solve(spectral, to_modes, from_modes, divisor)

    def clone(implicit):
        pieces = implicit.reshape(traj_count, -1, degree_count)
        spread = lax.all_to_all(pieces, "traj", split_axis=0, concat_axis=0, tiled=True)
        chosen = jnp.take(spread, sources, axis=0)
        merged = lax.all_to_all(chosen, "traj", split_axis=0, concat_axis=0, tiled=True)
        return merged.reshape(implicit.shape)

    def to_band_grid(implicit):
        band_parts = jnp.einsum(
            "mjn,pmln->ljpm", legendre, implicit, preferred_element_type=jnp.float32
        )
        band_parts = band_parts.astype(jnp.bfloat16)
        band_parts = band_parts.reshape(band_parts.shape[0], band_parts.shape[1], 2 * local_waves)
        return to_grid(lax.all_to_all(band_parts, "lat", split_axis=1, concat_axis=2, tiled=True))

    state_grid = ensemble[0]
    level_count, row_count, col_count = state_grid.shape
    width = 2 * local_waves
    block = 16
    if width % 128 or row_count % block:
        implicit = clone(to_implicit(grid_section(state_grid, mixing, lat_scale, forward)))
        state_grid = to_band_grid(implicit)
        state_grid = to_band_grid(
            to_implicit(grid_section(state_grid, mixing, lat_scale, forward))
        )
        return state_grid[None]

    mixer = spread_mixing(mixing)
    scale = jnp.broadcast_to(lat_scale[:, None], (row_count, 128))
    coeff_shape = (lat_count, level_count, row_count, width)

    def swap(blocks):
        return lax.all_to_all(blocks, "lat", split_axis=0, concat_axis=0, tiled=True)

    def solve(blocks):
        rows = blocks.transpose(1, 0, 2, 3).reshape(level_count, lat_count * row_count, width)
        return implicit_solve(to_spectral(rows), to_modes, from_modes, divisor)

    def bands_of(implicit):
        band_parts = jnp.einsum(
            "mjn,pmln->ljpm", legendre, implicit, preferred_element_type=jnp.float32
        ).astype(jnp.bfloat16)
        band_parts = band_parts.reshape(level_count, lat_count, row_count, width)
        return band_parts.transpose(1, 0, 2, 3)

    coefficients = row_call(
        first_kernel,
        (state_grid, mixer, scale, forward),
        (1, None, 0, None),
        coeff_shape,
        2,
        jnp.bfloat16,
        block,
    )
    bands = swap(bands_of(clone(solve(swap(coefficients)))))
    coefficients = row_call(
        middle_kernel,
        (bands, backward, mixer, scale, forward),
        (2, None, None, 0, None),
        coeff_shape,
        2,
        jnp.bfloat16,
        block,
    )
    bands = swap(bands_of(solve(swap(coefficients))))
    state_grid = row_call(
        last_kernel,
        (bands, backward),
        (2, None),
        state_grid.shape,
        1,
        jnp.float32,
        block,
    )
    return state_grid[None]


def solution(mesh):
    placed = (
        P("traj", None, "lat", None),
        P("traj"),
        P(),
        P("lat"),
        P("lat", None, None),
        P(),
        P(),
        P(),
    )
    return jax.shard_map(
        local, mesh=mesh, in_specs=placed, out_specs=P("traj", None, "lat", None), check_vma=False
    )
```

profile of v0, /device:TPU:0, one launch (start us, length us, event | category | flops | bytes accessed | tf_op | source)
XLA Modules:
  0.0 392.3 jit_solution(16423689108914164855)
XLA Ops:
  0.0 0.8 broadcast_multiply_fusion.1
  0.8 4.1 %broadcast_multiply_fusion = bf16[56,8,56,8]{3,2,1,0:T(8,128)(2,1)} fusion(bf16[8,8]{1,0:T(8,128)(2,1)S(1)} %fusion.52, bf16[56,56]{1,0:T(8,128)(2,1)} %param.10), kind=kLoop, calls=%fused_computation.16 | loop fusion | flops 200704 | bytes 407808 | tf_op jit(solution)/shard_map/jit(kron)/mul | solution.py:68
  4.9 7.8 %mul.128.mixer_ref = bf16[448,448]{1,0:T(8,128)(2,1)} reshape(bf16[56,8,56,8]{3,2,1,0:T(8,128)(2,1)} %broadcast_multiply_fusion) | data formatting | bytes 802816 | tf_op jit(solution)/shard_map/jit(kron)/mul | solution.py:68
  12.7 1.7 select_convert_fusion.forward_ref
  14.5 3.4 copy-done.2
  17.8 1.0 copy-done.3
  18.8 6.9 %shard_map.82 = bf16[2,56,96,128]{3,2,1,0:T(8,128)(2,1)S(1)} custom-call(f32[56,96,384]{2,1,0:T(8,128)S(1)} %bitcast.80, bf16[448,448]{1,0:T(8,128)(2,1)S(1)} %copy-done.3, f32[96,128]{1,0:T(8,128)S(1)} %broadcast_in_dim.58.scale_ref, bf16[384,256]{1,0:T(8,128)(2,1)S(1)} %select_convert_fusion.forward_ref), custom_call_target="tpu_custom_call" | custom-call | tf_op jit(solution)/shard_map/pallas_call | solution.py:138
  25.7 1.5 copy-done.1
  27.3 0.6 copy-done.5
  27.9 5.2 %all-to-all-start = ((bf16[2,56,96,128]{3,2,1,0:T(8,128)(2,1)}), bf16[2,56,96,128]{3,2,1,0:T(8,128)(2,1)}, u32[]{:S(2)}, u32[]{:S(2)}) async-start(bf16[2,56,96,128]{3,2,1,0:T(8,128)(2,1)} %copy-done.1), calls=%async_computation | async-start | bytes 5505024 | tf_op jit(solution)/shard_map/all_to_all | solution.py:213
  33.2 33.3 %all-to-all-done = bf16[2,56,96,128]{3,2,1,0:T(8,128)(2,1)} async-done(((bf16[2,56,96,128]{3,2,1,0:T(8,128)(2,1)}), bf16[2,56,96,128]{3,2,1,0:T(8,128)(2,1)}, u32[]{:S(2)}, u32[]{:S(2)}) %all-to-all-start) | async-done | bytes 2752544 | tf_op jit(solution)/shard_map/all_to_all | solution.py:213
  66.5 8.9 %copy.22 = bf16[56,2,96,128]{2,1,3,0:T(2,128)(2,1)} copy(bf16[56,2,96,128]{3,2,0,1:T(8,128)(2,1)} %bitcast.4) | data formatting | bytes 5505024 | tf_op jit(solution)/shard_map/transpose | solution.py:216
  75.4 6.9 %reshape_reshape.6 = bf16[56,192,2,64]{1,3,2,0:T(8,128)(2,1)} reshape(bf16[56,2,96,128]{2,1,3,0:T(2,128)(2,1)} %copy.22) | data formatting | bytes 5505024 | tf_op jit(solution)/shard_map/reshape;reshape | solution.py:165
  82.2 4.6 %fusion.21 = f32[2,64,56,128]{3,2,0,1:T(8,128)S(1)} fusion(bf16[64,192,128]{2,1,0:T(8,128)(2,1)S(1)} %copy-done, bf16[56,192,2,64]{1,3,2,0:T(8,128)(2,1)} %reshape_reshape.6), kind=kOutput, calls=%fused_computation.23 | convolution fusion | flops 352321536 | bytes 9568256 | tf_op jit(solution)/shard_map/ljpm,mjn->pmln/dot_general | solution.py:166
  86.8 3.6 fusion.7
  90.5 4.7 %fusion.37 = bf16[2,64,128,56]{2,3,1,0:T(8,128)(2,1)} fusion(f32[2,64,128,56]{2,3,1,0:T(8,128)S(1)} %fusion.7, f32[56,128]{1,0:T(8,128)S(1)} %multiply_add_fusion, f32[56,56]{1,0:T(8,128)S(1)} %copy-done.7), kind=kOutput, calls=%fused_computation.30 | convolution fusion | flops 618397696 | bytes 5546240 | tf_op jit(solution)/shard_map/lk,pmkn->pmln/dot_general | solution.py:62
  95.1 6.3 %all-to-all-start.1 = ((bf16[16,448,128]{2,1,0:T(8,128)(2,1)}), bf16[16,448,128]{2,1,0:T(8,128)(2,1)}, u32[]{:S(2)}, u32[]{:S(2)}) async-start(bf16[16,448,128]{2,1,0:T(8,128)(2,1)} %bitcast.85), calls=%async_computation.1 | async-start | bytes 3670016 | tf_op jit(solution)/shard_map/all_to_all | solution.py:183
  102.1 0.6 dynamic-slice
  102.7 0.9 dynamic-update-slice
  103.6 41.4 %all-reduce = s32[16]{0:T(128)S(1)} all-reduce(s32[16]{0:T(128)S(1)} %dynamic-update-slice), channel_id=1, replica_groups=mesh['traj'=16,'lat'=2] {'traj'}, use_global_device_ids=true, to_apply=%add | all-reduce | flops 16 | bytes 128
  145.2 0.1 reduce.1
  145.4 0.1 reduce
  145.6 0.2 convert_reduce_fusion
  145.8 3.5 gather_fusion
  149.3 1.7 broadcast_select_fusion
  151.0 46.3 %all_to_all.30 = bf16[16,448,128]{2,1,0:T(8,128)(2,1)S(1)} all-to-all(bf16[16,448,128]{2,1,0:T(8,128)(2,1)S(1)} %broadcast_select_fusion), channel_id=1, replica_groups=mesh['traj'=16,'lat'=2] {'traj'}, dimensions={0} | all-to-all | bytes 3670016 | tf_op jit(solution)/shard_map/all_to_all | solution.py:185
  197.3 2.2 convert_bitcast_fusion.1
  199.5 3.2 copy.26
  202.7 6.9 %reshape.181 = bf16[56,2,96,128]{2,1,3,0:T(2,128)(2,1)} reshape(bf16[56,192,2,64]{1,3,2,0:T(8,128)(2,1)} %copy.26) | data formatting | bytes 5505024 | tf_op jit(solution)/shard_map/reshape | solution.py:223
  209.5 8.7 %copy.27 = bf16[56,2,96,128]{3,2,0,1:T(8,128)(2,1)} copy(bf16[56,2,96,128]{2,1,3,0:T(2,128)(2,1)} %reshape.181) | data formatting | bytes 5505024 | tf_op jit(solution)/shard_map/reshape | solution.py:223
  218.2 5.1 %all-to-all-start.3 = ((bf16[2,56,96,128]{3,2,1,0:T(8,128)(2,1)}), bf16[2,56,96,128]{3,2,1,0:T(8,128)(2,1)}, u32[]{:S(2)}, u32[]{:S(2)}) async-start(bf16[2,56,96,128]{3,2,1,0:T(8,128)(2,1)} %bitcast.81), calls=%async_computation.3 | async-start | bytes 5505024 | tf_op jit(solution)/shard_map/all_to_all | solution.py:213
  223.3 2.0 multiply_convert_fusion.backward_ref
  225.3 31.2 %all-to-all-done.3.bands_ref = bf16[2,56,96,128]{3,2,1,0:T(8,128)(2,1)} async-done(((bf16[2,56,96,128]{3,2,1,0:T(8,128)(2,1)}), bf16[2,56,96,128]{3,2,1,0:T(8,128)(2,1)}, u32[]{:S(2)}, u32[]{:S(2)}) %all-to-all-start.3) | async-done | bytes 2752544 | tf_op jit(solution)/shard_map/all_to_all | solution.py:213
  256.5 1.0 copy-done.4
  257.5 0.8 copy-done.6
  258.3 9.4 %shard_map.83 = bf16[2,56,96,128]{3,2,1,0:T(8,128)(2,1)S(1)} custom-call(bf16[2,56,96,128]{3,2,1,0:T(8,128)(2,1)} %all-to-all-done.3.bands_ref, bf16[256,384]{1,0:T(8,128)(2,1)S(1)} %multiply_convert_fusion.backward_ref, bf16[448,448]{1,0:T(8,128)(2,1)S(1)} %copy-done.4, f32[96,128]{1,0:T(8,128)S(1)} %copy-done.6, ...), custom_call_target="tpu_custom_call" | custom-call | tf_op jit(solution)/shard_map/pallas_call | solution.py:138
  267.7 35.7 %all_to_all.31 = bf16[2,56,96,128]{3,2,1,0:T(8,128)(2,1)} all-to-all(bf16[2,56,96,128]{3,2,1,0:T(8,128)(2,1)S(1)} %shard_map.83), channel_id=1, replica_groups=mesh['traj'=16,'lat'=2] {'lat'}, dimensions={0} | all-to-all | bytes 5505024 | tf_op jit(solution)/shard_map/all_to_all | solution.py:213
  303.5 8.9 %copy.28 = bf16[56,2,96,128]{2,1,3,0:T(2,128)(2,1)} copy(bf16[56,2,96,128]{3,2,0,1:T(8,128)(2,1)} %bitcast.82) | data formatting | bytes 5505024 | tf_op jit(solution)/shard_map/transpose | solution.py:216
  312.3 6.9 %reshape_reshape.7 = bf16[56,192,2,64]{1,3,2,0:T(8,128)(2,1)} reshape(bf16[56,2,96,128]{2,1,3,0:T(2,128)(2,1)} %copy.28) | data formatting | bytes 5505024 | tf_op jit(solution)/shard_map/reshape;reshape | solution.py:165
  319.2 4.6 %fusion.26 = f32[2,64,56,128]{3,2,0,1:T(8,128)S(1)} fusion(bf16[64,192,128]{2,1,0:T(8,128)(2,1)S(1)} %copy-done, bf16[56,192,2,64]{1,3,2,0:T(8,128)(2,1)} %reshape_reshape.7), kind=kOutput, calls=%fused_computation.24 | convolution fusion | flops 352321536 | bytes 9568256 | tf_op jit(solution)/shard_map/ljpm,mjn->pmln/dot_general | solution.py:166
  323.8 3.7 bitcast_divide_fusion
  327.5 3.4 fusion.1
  330.9 2.1 convert_bitcast_fusion
  333.0 3.1 copy.32
  336.1 6.9 %reshape.182 = bf16[56,2,96,128]{2,1,3,0:T(2,128)(2,1)} reshape(bf16[56,192,2,64]{1,3,2,0:T(8,128)(2,1)} %copy.32) | data formatting | bytes 5505024 | tf_op jit(solution)/shard_map/reshape | solution.py:223
  343.0 8.7 %copy.33 = bf16[56,2,96,128]{3,2,0,1:T(8,128)(2,1)} copy(bf16[56,2,96,128]{2,1,3,0:T(2,128)(2,1)} %reshape.182) | data formatting | bytes 5505024 | tf_op jit(solution)/shard_map/reshape | solution.py:223
  351.7 35.2 %all_to_all.32.bands_ref = bf16[2,56,96,128]{3,2,1,0:T(8,128)(2,1)S(1)} all-to-all(bf16[2,56,96,128]{3,2,1,0:T(8,128)(2,1)} %bitcast.83), channel_id=1, replica_groups=mesh['traj'=16,'lat'=2] {'lat'}, dimensions={0} | all-to-all | bytes 5505024 | tf_op jit(solution)/shard_map/all_to_all | solution.py:213
  386.9 5.4 %shard_map.84 = f32[56,96,384]{2,1,0:T(8,128)} custom-call(bf16[2,56,96,128]{3,2,1,0:T(8,128)(2,1)S(1)} %all_to_all.32.bands_ref, bf16[256,384]{1,0:T(8,128)(2,1)S(1)} %multiply_convert_fusion.backward_ref), custom_call_target="tpu_custom_call" | custom-call | tf_op jit(solution)/shard_map/pallas_call | solution.py:138
  (41 shorter events, 0.5 us)
Async XLA Ops:
  0.0 82.2 %copy-start = (bf16[64,192,128]{2,1,0:T(8,128)(2,1)S(1)}, bf16[64,192,128]{2,1,0:T(8,128)(2,1)}, u32[]{:S(2)}) copy-start(bf16[64,192,128]{2,1,0:T(8,128)(2,1)} %param.12) | copy-start | bytes 9437188
  14.5 3.4 copy-start.2
  17.8 1.0 copy-start.3
  25.7 1.5 copy-start.1
  27.3 0.6 copy-start.5
  27.9 5.2 %copy-start.13 = (f32[56]{0:T(128)S(1)}, f32[56]{0:T(128)}, u32[]{:S(2)}) copy-start(f32[56]{0:T(128)} %param.15) | copy-start | bytes 676
  27.9 38.6 %all-to-all-start = ((bf16[2,56,96,128]{3,2,1,0:T(8,128)(2,1)}), bf16[2,56,96,128]{3,2,1,0:T(8,128)(2,1)}, u32[]{:S(2)}, u32[]{:S(2)}) async-start(bf16[2,56,96,128]{3,2,1,0:T(8,128)(2,1)} %copy-done.1), calls=%async_computation | async-start | bytes 5505024 | tf_op jit(solution)/shard_map/all_to_all | solution.py:213
  33.2 57.3 %copy-start.9 = (f32[56,128]{1,0:T(8,128)}, f32[56,128]{1,0:T(8,128)S(1)}, u32[]{:S(2)}) copy-start(f32[56,128]{1,0:T(8,128)S(1)} %multiply_add_fusion) | copy-start | bytes 86020
  82.2 4.6 %copy-start.11 = (f32[56,56]{1,0:T(8,128)S(1)}, f32[56,56]{1,0:T(8,128)}, u32[]{:S(2)}) copy-start(f32[56,56]{1,0:T(8,128)} %param.13) | copy-start | bytes 37636
  86.8 3.7 copy-start.7
  95.1 7.0 %copy-start.14 = (u32[32]{0:T(128)S(1)}, u32[32]{0:T(128)}, u32[]{:S(2)}) copy-start(u32[32]{0:T(128)} %constant.108) | copy-start | bytes 388
  95.1 50.6 %all-to-all-start.1 = ((bf16[16,448,128]{2,1,0:T(8,128)(2,1)}), bf16[16,448,128]{2,1,0:T(8,128)(2,1)}, u32[]{:S(2)}, u32[]{:S(2)}) async-start(bf16[16,448,128]{2,1,0:T(8,128)(2,1)} %bitcast.85), calls=%async_computation.1 | async-start | bytes 3670016 | tf_op jit(solution)/shard_map/all_to_all | solution.py:183
  218.2 38.2 %all-to-all-start.3 = ((bf16[2,56,96,128]{3,2,1,0:T(8,128)(2,1)}), bf16[2,56,96,128]{3,2,1,0:T(8,128)(2,1)}, u32[]{:S(2)}, u32[]{:S(2)}) async-start(bf16[2,56,96,128]{3,2,1,0:T(8,128)(2,1)} %bitcast.81), calls=%async_computation.3 | async-start | bytes 5505024 | tf_op jit(solution)/shard_map/all_to_all | solution.py:213
  256.5 1.0 copy-start.4
  257.5 0.8 copy-start.6
  319.2 4.6 %copy-start.10 = (f32[56,128]{1,0:T(8,128)S(1)}, f32[56,128]{1,0:T(8,128)}, u32[]{:S(2)}) copy-start(f32[56,128]{1,0:T(8,128)} %copy-done.9) | copy-start | bytes 86020
  319.2 4.6 %copy-start.12 = (f32[56,56]{1,0:T(8,128)S(1)}, f32[56,56]{1,0:T(8,128)}, u32[]{:S(2)}) copy-start(f32[56,56]{1,0:T(8,128)} %param.13) | copy-start | bytes 37636
  323.8 3.7 copy-start.8
where the time goes:
time: 395 us; the launch traced here: 392 us
  blocking collectives  159 us (40%)
  local copies, waits for them, and re-layouts  90.3 us (23%)
  waiting for transfers between devices  64.5 us (16%)
  matrix products  28.8 us (7%)
  Pallas kernels  21.7 us (5%)
  starting transfers between devices  16.6 us (4%)
  other arithmetic  10.9 us (3%)
    all_to_all x2, blocking collectives, swap(): lax.all_to_all(blocks, 'lat', split_axis=0, concat_axis=0, tiled=True)  70.9 us
    all_to_all x2, waiting for transfers between devices, swap(): lax.all_to_all(blocks, 'lat', split_axis=0, concat_axis=0, tiled=True)  64.5 us
    all_to_all x1, blocking collectives, clone(): lax.all_to_all(chosen, 'traj', split_axis=0, concat_axis=0, tiled=True)  46.3 us
    unnamed x1, blocking collectives  41.4 us
    reshape x4, local copies, waits for them, and re-layouts, bands_of(): band_parts = band_parts.reshape(level_count, lat_count, row_count, width)  31.1 us
    pallas_call x3, Pallas kernels, row_call(): pl.pallas_call(kernel, grid=(rows // block,), in_specs=specs, out_specs=b...  21.7 us
    transpose x2, local copies, waits for them, and re-layouts, solve(): blocks.transpose(1, 0, 2, 3)  17.7 us
    another operation x2, local copies, waits for them, and re-layouts, to_spectral(): received.reshape(received.shape[0], received.shape[1], 2, local_waves)  13.7 us
  transfers between devices with their start and end apart: 3, of which 2 were waited for; matrix products, arithmetic and copies ran while one was open for 1% of the time, Pallas kernels for 0%

commit v1 on v0

--- a/solution.py
+++ b/solution.py
@@ -65,7 +65,13 @@
 
 
 def spread_mixing(mixing):
-    return jnp.kron(mixing, jnp.eye(8, dtype=mixing.dtype))
+    level_count = mixing.shape[0]
+    at = jnp.arange(8 * level_count, dtype=jnp.int32)
+    picks = (at[:, None] // 8 == jnp.arange(level_count)[None, :]).astype(mixing.dtype)
+    tall = jnp.dot(picks, mixing, preferred_element_type=jnp.float32).astype(mixing.dtype)
+    both = jnp.dot(tall, picks.T, preferred_element_type=jnp.float32)
+    same_row = at[:, None] % 8 == at[None, :] % 8
+    return jnp.where(same_row, both, 0.0).astype(mixing.dtype)
 
 
 def to_coefficients(values, mixer, scale, forward):
@@ -154,8 +160,14 @@
     longitudes = ensemble.shape[3]
     columns = jnp.arange(2 * total_waves, dtype=jnp.int32)
     within = columns % (2 * local_waves)
-    wavenumber = columns // (2 * local_waves) * local_waves + within % local_waves
-    component = within // local_waves
+    width = 2 * local_waves
+    block = 16
+    whole_blocks = width % 128 == 0 and ensemble.shape[2] % block == 0
+    if whole_blocks:
+        wave_of, component = within // 2, within % 2
+    else:
+        wave_of, component = within % local_waves, within // local_waves
+    wavenumber = columns // width * local_waves + wave_of
     forward, backward = fourier_tables(wavenumber, component, longitudes)
     lat_scale = weights / longitudes
     divisor = mode_divisor(mode_rates, degree_count)
@@ -195,9 +207,7 @@
 
     state_grid = ensemble[0]
     level_count, row_count, col_count = state_grid.shape
-    width = 2 * local_waves
-    block = 16
-    if width % 128 or row_count % block:
+    if not whole_blocks:
         implicit = clone(to_implicit(grid_section(state_grid, mixing, lat_scale, forward)))
         state_grid = to_band_grid(implicit)
         state_grid = to_band_grid(
@@ -212,16 +222,30 @@
     def swap(blocks):
         return lax.all_to_all(blocks, "lat", split_axis=0, concat_axis=0, tiled=True)
 
+    tables = legendre.reshape(local_waves, lat_count, row_count, degree_count)
+
     def solve(blocks):
-        rows = blocks.transpose(1, 0, 2, 3).reshape(level_count, lat_count * row_count, width)
-        return implicit_solve(to_spectral(rows), to_modes, from_modes, divisor)
+        columns_first = lax.optimization_barrier(blocks.transpose(0, 3, 1, 2))
+        rows = columns_first.reshape(lat_count, local_waves, 2 * level_count, row_count)
+        spectral = sum(
+            jnp.einsum(
+                "mrj,mjn->mrn", rows[part], tables[:, part], preferred_element_type=jnp.float32
+            )
+            for part in range(lat_count)
+        )
+        spectral = spectral.reshape(1, width, level_count, degree_count)
+        return implicit_solve(spectral, to_modes, from_modes, divisor)
 
     def bands_of(implicit):
-        band_parts = jnp.einsum(
-            "mjn,pmln->ljpm", legendre, implicit, preferred_element_type=jnp.float32
-        ).astype(jnp.bfloat16)
-        band_parts = band_parts.reshape(level_count, lat_count, row_count, width)
-        return band_parts.transpose(1, 0, 2, 3)
+        rows = implicit.reshape(local_waves, 2 * level_count, degree_count)
+        parts = [
+            jnp.einsum(
+                "mrn,mjn->mrj", rows, tables[:, part], preferred_element_type=jnp.float32
+            ).astype(jnp.bfloat16)
+            for part in range(lat_count)
+        ]
+        columns_first = jnp.stack(parts).reshape(lat_count, width, level_count, row_count)
+        return lax.optimization_barrier(columns_first).transpose(0, 2, 3, 1)
 
     coefficients = row_call(
         first_kernel,

time: 395 us -> 353 us (0.89)
  local copies, waits for them, and re-layouts: 90.3 us -> 47.1 us
  matrix products: 28.8 us -> 33.8 us
    reshape x4 -> x0, local copies, waits for them, and re-layouts: 31.1 us -> none  [bands_of(): band_parts = band_parts.reshape(level_count, lat_count, row_count, width)]
    transpose x2 -> x0, local copies, waits for them, and re-layouts: 17.7 us -> none  [solve(): blocks.transpose(1, 0, 2, 3)]
    slice x0 -> x6, local copies, waits for them, and re-layouts: none -> 15.4 us  [solve(): rows[part]]
    mul x1 -> x0, local copies, waits for them, and re-layouts: 7.78 us -> none  [spread_mixing(): return jnp.kron(mixing, jnp.eye(8, dtype=mixing.dtype))]
    convert_element_type x2 -> x4, local copies, waits for them, and re-layouts: 6.35 us -> 12.9 us  [bands_of(): parts = [jnp.einsum('mrn,mjn->mrj', rows, tables[:, part], preferred_elem...]
    another operation x5 -> x7, other arithmetic: 0.32 us -> 5.86 us  [the longest x2 5.54 us: bands_of(): jnp.stack(parts).reshape(lat_count, width, level_count, row_count)]
    dot_general x4 -> x9, matrix products: 13.4 us -> 18.5 us  [the longest x4 9.74 us: bands_of(): jnp.einsum('mrn,mjn->mrj', rows, tables[:, part], preferred_element_type=...]
    mul x1 -> x0, other arithmetic: 4.06 us -> none  [spread_mixing(): return jnp.kron(mixing, jnp.eye(8, dtype=mixing.dtype))]
where the time goes in v1:
time: 353 us; the launch traced here: 352 us
  blocking collectives  157 us (44%)
  waiting for transfers between devices  63.3 us (18%)
  local copies, waits for them, and re-layouts  47.1 us (13%)
  matrix products  33.8 us (10%)
  Pallas kernels  21.8 us (6%)
  starting transfers between devices  14.5 us (4%)
  other arithmetic  12.9 us (4%)
    all_to_all x2, blocking collectives, swap(): lax.all_to_all(blocks, 'lat', split_axis=0, concat_axis=0, tiled=True)  68.9 us
    all_to_all x2, waiting for transfers between devices, swap(): lax.all_to_all(blocks, 'lat', split_axis=0, concat_axis=0, tiled=True)  63.3 us
    all_to_all x1, blocking collectives, clone(): lax.all_to_all(chosen, 'traj', split_axis=0, concat_axis=0, tiled=True)  46.5 us
    unnamed x1, blocking collectives  41.7 us
    pallas_call x3, Pallas kernels, row_call(): pl.pallas_call(kernel, grid=(rows // block,), in_specs=specs, out_specs=b...  21.8 us
    slice x6, local copies, waits for them, and re-layouts, solve(): rows[part]  15.4 us
    convert_element_type x4, local copies, waits for them, and re-layouts, bands_of(): parts = [jnp.einsum('mrn,mjn->mrj', rows, tables[:, part], preferred_elem...  12.9 us
    another operation x4, local copies, waits for them, and re-layouts, bands_of(): jnp.stack(parts).reshape(lat_count, width, level_count, row_count)  10.5 us
  transfers between devices with their start and end apart: 3, of which 2 were waited for; matrix products, arithmetic and copies ran while one was open for 1% of the time, Pallas kernels for 0%

profile of v1, /device:TPU:0, one launch (start us, length us, event | category | flops | bytes accessed | tf_op | source)
XLA Modules:
  0.0 351.6 jit_solution(9722770823303707098)
XLA Ops:
  0.7 1.7 select_convert_fusion.forward_ref
  2.4 1.3 fusion.14.mixer_ref
  3.8 3.4 copy-done.1
  7.1 7.7 %shard_map.82 = bf16[2,56,96,128]{3,2,1,0:T(8,128)(2,1)} custom-call(f32[56,96,384]{2,1,0:T(8,128)S(1)} %bitcast.98, bf16[448,448]{1,0:T(8,128)(2,1)S(1)} %fusion.14.mixer_ref, f32[96,128]{1,0:T(8,128)S(1)} %broadcast_in_dim.63.scale_ref, bf16[384,256]{1,0:T(8,128)(2,1)S(1)} %select_convert_fusion.forward_ref), custom_call_target="tpu_custom_call" | custom-call | tf_op jit(solution)/shard_map/pallas_call | solution.py:144
  14.8 4.4 %all-to-all-start = ((bf16[2,56,96,128]{3,2,1,0:T(8,128)(2,1)}), bf16[2,56,96,128]{3,2,1,0:T(8,128)(2,1)S(1)}, u32[]{:S(2)}, u32[]{:S(2)}) async-start(bf16[2,56,96,128]{3,2,1,0:T(8,128)(2,1)} %shard_map.82), calls=%async_computation | async-start | bytes 5505024 | tf_op jit(solution)/shard_map/all_to_all | solution.py:223
  19.3 32.9 %all-to-all-done = bf16[2,56,96,128]{3,2,1,0:T(8,128)(2,1)S(1)} async-done(((bf16[2,56,96,128]{3,2,1,0:T(8,128)(2,1)}), bf16[2,56,96,128]{3,2,1,0:T(8,128)(2,1)S(1)}, u32[]{:S(2)}, u32[]{:S(2)}) %all-to-all-start) | async-done | bytes 2752544 | tf_op jit(solution)/shard_map/all_to_all | solution.py:223
  52.2 1.7 fusion.49
  53.9 3.7 %copy.36 = bf16[1,128,56,96]{3,2,1,0:T(8,128)(2,1)} copy(bf16[1,128,56,96]{1,3,2,0:T(8,128)(2,1)} %get-tuple-element.9) | data formatting | bytes 2752512 | tf_op jit(solution)/shard_map/slice | solution.py:232
  57.6 2.9 copy.33
  60.5 2.7 fusion.16
  63.4 1.1 convolution_add_fusion.1
  64.6 3.4 fusion.33
  68.0 4.7 %fusion.8 = bf16[128,128,56]{1,2,0:T(8,128)(2,1)} fusion(f32[128,128,56]{1,2,0:T(8,128)S(1)} %fusion.33, f32[56,128]{1,0:T(8,128)S(1)} %multiply_add_fusion, f32[56,56]{1,0:T(8,128)S(1)} %copy-done.10), kind=kOutput, calls=%fused_computation.14 | convolution fusion | flops 618397696 | bytes 5546240 | tf_op jit(solution)/shard_map/lk,pmkn->pmln/dot_general | solution.py:62
  72.7 6.3 %all-to-all-start.1 = ((bf16[16,448,128]{2,1,0:T(8,128)(2,1)}), bf16[16,448,128]{2,1,0:T(8,128)(2,1)S(1)}, u32[]{:S(2)}, u32[]{:S(2)}) async-start(bf16[16,448,128]{2,1,0:T(8,128)(2,1)} %bitcast.125), calls=%async_computation.1 | async-start | bytes 3670016 | tf_op jit(solution)/shard_map/all_to_all | solution.py:195
  80.2 0.7 dynamic-update-slice
  80.9 41.7 %all-reduce = s32[16]{0:T(128)S(1)} all-reduce(s32[16]{0:T(128)S(1)} %dynamic-update-slice), channel_id=1, replica_groups=mesh['traj'=16,'lat'=2] {'traj'}, use_global_device_ids=true, to_apply=%add | all-reduce | flops 16 | bytes 128
  123.3 2.0 gather_fusion
  125.3 1.7 broadcast_select_fusion
  127.1 46.5 %all_to_all.30 = bf16[16,448,128]{2,1,0:T(8,128)(2,1)S(1)} all-to-all(bf16[16,448,128]{2,1,0:T(8,128)(2,1)S(1)} %broadcast_select_fusion), channel_id=1, replica_groups=mesh['traj'=16,'lat'=2] {'traj'}, dimensions={0} | all-to-all | bytes 3670016 | tf_op jit(solution)/shard_map/all_to_all | solution.py:197
  173.6 2.4 convolution_convert_fusion.2
  176.0 2.4 convolution_convert_fusion.3
  178.5 3.2 copy.39
  181.7 2.6 copy.41
  184.3 3.2 copy.40
  187.6 2.6 copy.42
  190.2 3.5 %pad_maximum_fusion = bf16[2,128,56,96]{1,3,2,0:T(8,128)(2,1)} fusion(bf16[1,128,56,96]{1,3,2,0:T(8,128)(2,1)} %copy.42, bf16[1,128,56,96]{1,3,2,0:T(8,128)(2,1)} %copy.41), kind=kLoop, calls=%fused_computation.7 | loop fusion | flops 1376256 | bytes 5505024 | tf_op jit(solution)/shard_map/stack | solution.py:247
  193.7 3.9 %all-to-all-start.3 = ((bf16[2,56,96,128]{3,2,1,0:T(8,128)(2,1)}), bf16[2,56,96,128]{3,2,1,0:T(8,128)(2,1)S(1)}, u32[]{:S(2)}, u32[]{:S(2)}) async-start(bf16[2,56,96,128]{3,2,1,0:T(8,128)(2,1)} %bitcast.112), calls=%async_computation.3 | async-start | bytes 5505024 | tf_op jit(solution)/shard_map/all_to_all | solution.py:223
  197.6 2.6 multiply_convert_fusion.backward_ref
  200.2 30.4 %all-to-all-done.3.bands_ref = bf16[2,56,96,128]{3,2,1,0:T(8,128)(2,1)S(1)} async-done(((bf16[2,56,96,128]{3,2,1,0:T(8,128)(2,1)}), bf16[2,56,96,128]{3,2,1,0:T(8,128)(2,1)S(1)}, u32[]{:S(2)}, u32[]{:S(2)}) %all-to-all-start.3) | async-done | bytes 2752544 | tf_op jit(solution)/shard_map/all_to_all | solution.py:223
  230.7 0.9 copy-done.2
  231.6 8.7 %shard_map.83 = bf16[2,56,96,128]{3,2,1,0:T(8,128)(2,1)S(1)} custom-call(bf16[2,56,96,128]{3,2,1,0:T(8,128)(2,1)S(1)} %all-to-all-done.3.bands_ref, bf16[256,384]{1,0:T(8,128)(2,1)S(1)} %copy-done.2, bf16[448,448]{1,0:T(8,128)(2,1)S(1)} %fusion.14.mixer_ref, f32[96,128]{1,0:T(8,128)S(1)} %broadcast_in_dim.63.scale_ref, ...), custom_call_target="tpu_custom_call" | custom-call | tf_op jit(solution)/shard_map/pallas_call | solution.py:144
  240.3 34.8 %all_to_all.31 = bf16[2,56,96,128]{3,2,1,0:T(8,128)(2,1)S(1)} all-to-all(bf16[2,56,96,128]{3,2,1,0:T(8,128)(2,1)S(1)} %shard_map.83), channel_id=1, replica_groups=mesh['traj'=16,'lat'=2] {'lat'}, dimensions={0} | all-to-all | bytes 5505024 | tf_op jit(solution)/shard_map/all_to_all | solution.py:223
  275.1 1.3 fusion.48
  276.4 2.9 copy.45
  279.2 2.9 copy.43
  282.2 2.7 fusion.15
  285.1 1.1 convolution_add_fusion
  286.2 3.6 %fusion.31 = f32[128,128,56]{1,2,0:T(8,128)S(1)} fusion(f32[128,56,128]{2,1,0:T(8,128)S(1)} %bitcast.110, f32[56,56]{1,0:T(8,128)S(1)} %copy-done), kind=kOutput, calls=%fused_computation.47 | convolution fusion | flops 616562688 | bytes 7352576 | tf_op jit(solution)/shard_map/kl,pmln->pmkn/dot_general | solution.py:59
  289.8 3.6 %fusion.11 = bf16[128,128,56]{1,2,0:T(8,128)(2,1)S(1)} fusion(f32[128,128,56]{1,2,0:T(8,128)S(1)} %fusion.31, f32[56,128]{1,0:T(8,128)S(1)} %multiply_add_fusion, f32[56,56]{1,0:T(8,128)S(1)} %copy-done.10), kind=kOutput, calls=%fused_computation.15 | convolution fusion | flops 618397696 | bytes 5546240 | tf_op jit(solution)/shard_map/lk,pmkn->pmln/dot_general | solution.py:62
  293.4 2.4 convolution_convert_fusion
  295.9 2.4 convolution_convert_fusion.1
  298.3 3.2 copy.47
  301.6 2.6 copy.49
  304.2 3.2 copy.48
  307.4 2.6 copy.50
  310.0 2.0 pad_maximum_fusion.1
  312.1 34.1 %all_to_all.32.bands_ref = bf16[2,56,96,128]{3,2,1,0:T(8,128)(2,1)S(1)} all-to-all(bf16[2,56,96,128]{3,2,1,0:T(8,128)(2,1)S(1)} %bitcast.114), channel_id=1, replica_groups=mesh['traj'=16,'lat'=2] {'lat'}, dimensions={0} | all-to-all | bytes 5505024 | tf_op jit(solution)/shard_map/all_to_all | solution.py:223
  346.1 5.4 %shard_map.84 = f32[56,96,384]{2,1,0:T(8,128)} custom-call(bf16[2,56,96,128]{3,2,1,0:T(8,128)(2,1)S(1)} %all_to_all.32.bands_ref, bf16[256,384]{1,0:T(8,128)(2,1)S(1)} %copy-done.3), custom_call_target="tpu_custom_call" | custom-call | tf_op jit(solution)/shard_map/pallas_call | solution.py:144
  (44 shorter events, 2.6 us)
Async XLA Ops:
  0.0 64.5 %copy-start = (f32[56,56]{1,0:T(8,128)S(1)}, f32[56,56]{1,0:T(8,128)}, u32[]{:S(2)}) copy-start(f32[56,56]{1,0:T(8,128)} %param.13) | copy-start | bytes 37636
  3.7 3.4 copy-start.1
  14.8 4.4 %copy-start.9 = (f32[56]{0:T(128)S(1)}, f32[56]{0:T(128)}, u32[]{:S(2)}) copy-start(f32[56]{0:T(128)} %param.15) | copy-start | bytes 676
  14.8 37.4 %all-to-all-start = ((bf16[2,56,96,128]{3,2,1,0:T(8,128)(2,1)}), bf16[2,56,96,128]{3,2,1,0:T(8,128)(2,1)S(1)}, u32[]{:S(2)}, u32[]{:S(2)}) async-start(bf16[2,56,96,128]{3,2,1,0:T(8,128)(2,1)} %shard_map.82), calls=%async_computation | async-start | bytes 5505024 | tf_op jit(solution)/shard_map/all_to_all | solution.py:223
  60.5 2.7 copy-start.4
  60.5 2.9 copy-start.7
  64.6 3.4 copy-start.10
  72.7 6.9 %copy-start.11 = (u32[32]{0:T(128)S(1)}, u32[32]{0:T(128)}, u32[]{:S(2)}) copy-start(u32[32]{0:T(128)} %constant.145) | copy-start | bytes 388
  72.7 50.6 %all-to-all-start.1 = ((bf16[16,448,128]{2,1,0:T(8,128)(2,1)}), bf16[16,448,128]{2,1,0:T(8,128)(2,1)S(1)}, u32[]{:S(2)}, u32[]{:S(2)}) async-start(bf16[16,448,128]{2,1,0:T(8,128)(2,1)} %bitcast.125), calls=%async_computation.1 | async-start | bytes 3670016 | tf_op jit(solution)/shard_map/all_to_all | solution.py:195
  127.1 46.5 %copy-start.5 = (bf16[64,192,128]{2,1,0:T(8,128)(2,1)S(1)}, bf16[64,192,128]{2,1,0:T(8,128)(2,1)}, u32[]{:S(2)}) copy-start(bf16[64,192,128]{2,1,0:T(8,128)(2,1)} %param.12) | copy-start | bytes 9437188
  193.7 36.9 %all-to-all-start.3 = ((bf16[2,56,96,128]{3,2,1,0:T(8,128)(2,1)}), bf16[2,56,96,128]{3,2,1,0:T(8,128)(2,1)S(1)}, u32[]{:S(2)}, u32[]{:S(2)}) async-start(bf16[2,56,96,128]{3,2,1,0:T(8,128)(2,1)} %bitcast.112), calls=%async_computation.3 | async-start | bytes 5505024 | tf_op jit(solution)/shard_map/all_to_all | solution.py:223
  230.7 0.9 copy-start.2
  282.2 2.7 copy-start.6
  282.2 2.9 copy-start.8
  312.0 34.1 %copy-start.3 = (bf16[256,384]{1,0:T(8,128)(2,1)S(1)}, bf16[256,384]{1,0:T(8,128)(2,1)}, u32[]{:S(2)}) copy-start(bf16[256,384]{1,0:T(8,128)(2,1)} %multiply_convert_fusion.backward_ref) | copy-start | bytes 589828

commit v2 on v1

--- a/solution.py
+++ b/solution.py
@@ -1,3 +1,4 @@
+import functools
 import math
 
 import jax
@@ -84,11 +85,11 @@
 
 
 def from_bands(bands, backward):
-    parts, level_count, rows, width = bands.shape
+    level_count, rows, width = bands[0].shape
     total = None
-    for part in range(parts):
+    for part, band in enumerate(bands):
         term = jnp.dot(
-            bands[part].astype(jnp.bfloat16).reshape(level_count * rows, width),
+            band[...].reshape(level_count * rows, width),
             backward[part * width : (part + 1) * width, :],
             preferred_element_type=jnp.float32,
         )
@@ -96,34 +97,35 @@
     return total.reshape(level_count, rows, backward.shape[1])
 
 
-def split_columns(pieces, out_ref):
+def split_columns(pieces, out_refs):
     whole = jnp.concatenate(pieces, axis=1)
-    width = out_ref.shape[3]
-    for part in range(out_ref.shape[0]):
-        out_ref[part] = whole[:, :, part * width : (part + 1) * width].astype(jnp.bfloat16)
-
-
-def first_kernel(grid_ref, mixer_ref, scale_ref, forward_ref, out_ref):
+    width = out_refs[0].shape[2]
+    for part, out_ref in enumerate(out_refs):
+        out_ref[...] = whole[:, :, part * width : (part + 1) * width].astype(jnp.bfloat16)
+
+
+def first_kernel(grid_ref, mixer_ref, scale_ref, forward_ref, *out_refs):
     pieces = []
     for low in range(0, grid_ref.shape[1], 8):
         values = grid_ref[:, low : low + 8, :]
         scale = scale_ref[low : low + 8, :]
         pieces.append(to_coefficients(values, mixer_ref[...], scale, forward_ref[...]))
-    split_columns(pieces, out_ref)
-
-
-def middle_kernel(bands_ref, backward_ref, mixer_ref, scale_ref, forward_ref, out_ref):
-    whole = from_bands(bands_ref[...], backward_ref[...])
+    split_columns(pieces, out_refs)
+
+
+def middle_kernel(parts, backward_ref, mixer_ref, scale_ref, forward_ref, *refs):
+    out_refs = refs[parts:]
+    whole = from_bands(refs[:parts], backward_ref[...])
     pieces = []
     for low in range(0, whole.shape[1], 8):
         scale = scale_ref[low : low + 8, :]
         values = whole[:, low : low + 8, :]
         pieces.append(to_coefficients(values, mixer_ref[...], scale, forward_ref[...]))
-    split_columns(pieces, out_ref)
-
-
-def last_kernel(bands_ref, backward_ref, out_ref):
-    out_ref[...] = from_bands(bands_ref[...], backward_ref[...])
+    split_columns(pieces, out_refs)
+
+
+def last_kernel(backward_ref, *refs):
+    refs[-1][...] = from_bands(refs[:-1], backward_ref[...])
 
 
 def fixed(array):
@@ -135,8 +137,8 @@
     return pl.BlockSpec(sizes, lambda step: tuple(step if at == axis else 0 for at in range(len(shape))))
 
 
-def row_call(kernel, operands, row_axes, out_shape, out_axis, out_type, block):
-    rows = out_shape[out_axis]
+def row_call(kernel, operands, row_axes, out_shape, out_count, out_type, block):
+    rows = out_shape[1]
     specs = [
         fixed(op) if axis is None else by_rows(op.shape, axis, block)
         for op, axis in zip(operands, row_axes)
@@ -145,8 +147,8 @@
         kernel,
         grid=(rows // block,),
         in_specs=specs,
-        out_specs=by_rows(out_shape, out_axis, block),
-        out_shape=jax.ShapeDtypeStruct(out_shape, out_type),
+        out_specs=[by_rows(out_shape, 1, block)] * out_count,
+        out_shape=[jax.ShapeDtypeStruct(out_shape, out_type)] * out_count,
         compiler_params=pltpu.CompilerParams(vmem_limit_bytes=40 * 1024 * 1024),
     )(*operands)
 
@@ -217,60 +219,76 @@
 
     mixer = spread_mixing(mixing)
     scale = jnp.broadcast_to(lat_scale[:, None], (row_count, 128))
-    coeff_shape = (lat_count, level_count, row_count, width)
-
-    def swap(blocks):
-        return lax.all_to_all(blocks, "lat", split_axis=0, concat_axis=0, tiled=True)
-
+    coeff_shape = (level_count, row_count, width)
+    me = lax.axis_index("lat")
+    shifts = range(lat_count)
     tables = legendre.reshape(local_waves, lat_count, row_count, degree_count)
 
+    def take(array, part, axis):
+        return lax.dynamic_index_in_dim(array, part % lat_count, axis, keepdims=False)
+
+    send_tables = [take(tables, me + shift, 1) for shift in shifts]
+    recv_tables = [take(tables, me - shift + lat_count, 1) for shift in shifts]
+    forward_parts = forward.reshape(longitudes, lat_count, width)
+    forward = jnp.concatenate([take(forward_parts, me + shift, 1) for shift in shifts], axis=1)
+    backward_parts = backward.reshape(lat_count, width, longitudes)
+    backward = jnp.concatenate(
+        [take(backward_parts, me - shift + lat_count, 0) for shift in shifts], axis=0
+    )
+
+    def send(array, shift):
+        if shift == 0:
+            return array
+        pairs = [(at, (at + shift) % lat_count) for at in range(lat_count)]
+        return lax.ppermute(array, "lat", pairs)
+
     def solve(blocks):
-        columns_first = lax.optimization_barrier(blocks.transpose(0, 3, 1, 2))
-        rows = columns_first.reshape(lat_count, local_waves, 2 * level_count, row_count)
-        spectral = sum(
-            jnp.einsum(
-                "mrj,mjn->mrn", rows[part], tables[:, part], preferred_element_type=jnp.float32
+        spectral = 0.0
+        for shift in shifts:
+            arrived = send(blocks[shift], shift)
+            rows = lax.optimization_barrier(arrived.transpose(2, 0, 1))
+            rows = rows.reshape(local_waves, 2 * level_count, row_count)
+            spectral += jnp.einsum(
+                "mrj,mjn->mrn", rows, recv_tables[shift], preferred_element_type=jnp.float32
             )
-            for part in range(lat_count)
-        )
         spectral = spectral.reshape(1, width, level_count, degree_count)
         return implicit_solve(spectral, to_modes, from_modes, divisor)
 
     def bands_of(implicit):
         rows = implicit.reshape(local_waves, 2 * level_count, degree_count)
-        parts = [
-            jnp.einsum(
-                "mrn,mjn->mrj", rows, tables[:, part], preferred_element_type=jnp.float32
+        result = []
+        for shift in shifts:
+            part = jnp.einsum(
+                "mrn,mjn->mrj", rows, send_tables[shift], preferred_element_type=jnp.float32
             ).astype(jnp.bfloat16)
-            for part in range(lat_count)
-        ]
-        columns_first = jnp.stack(parts).reshape(lat_count, width, level_count, row_count)
-        return lax.optimization_barrier(columns_first).transpose(0, 2, 3, 1)
+            part = lax.optimization_barrier(part.reshape(width, level_count, row_count))
+            result.append(send(part.transpose(1, 2, 0), shift))
+        return result
 
     coefficients = row_call(
         first_kernel,
         (state_grid, mixer, scale, forward),
         (1, None, 0, None),
         coeff_shape,
-        2,
+        lat_count,
         jnp.bfloat16,
         block,
     )
-    bands = swap(bands_of(clone(solve(swap(coefficients)))))
+    bands = bands_of(clone(solve(coefficients)))
     coefficients = row_call(
-        middle_kernel,
-        (bands, backward, mixer, scale, forward),
-        (2, None, None, 0, None),
+        functools.partial(middle_kernel, lat_count),
+        (backward, mixer, scale, forward, *bands),
+        (None, None, 0, None) + (1,) * lat_count,
         coeff_shape,
-        2,
+        lat_count,
         jnp.bfloat16,
         block,
     )
-    bands = swap(bands_of(solve(swap(coefficients))))
-    state_grid = row_call(
+    bands = bands_of(solve(coefficients))
+    (state_grid,) = row_call(
         last_kernel,
-        (bands, backward),
-        (2, None),
+        (backward, *bands),
+        (None,) + (1,) * lat_count,
         state_grid.shape,
         1,
         jnp.float32,

time: 353 us -> 328 us (0.929)
  blocking collectives: 157 us -> 88 us
  waiting for transfers between devices: 63.3 us -> 81.5 us
  local copies, waits for them, and re-layouts: 47.1 us -> 63.9 us
  matrix products: 33.8 us -> 46.7 us
  other arithmetic: 12.9 us -> 6.86 us
    ppermute x0 -> x4, waiting for transfers between devices: none -> 81.5 us  [send(): return lax.ppermute(array, 'lat', pairs)]
    all_to_all x2 -> x0, blocking collectives: 68.9 us -> none  [swap(): lax.all_to_all(blocks, 'lat', split_axis=0, concat_axis=0, tiled=True)]
    all_to_all x2 -> x0, waiting for transfers between devices: 63.3 us -> none  [swap(): lax.all_to_all(blocks, 'lat', split_axis=0, concat_axis=0, tiled=True)]
    optimization_barrier x0 -> x8, local copies, waits for them, and re-layouts: none -> 30.1 us  [the longest x4 15.2 us: bands_of(): part = lax.optimization_barrier(part.reshape(width, level_count, row_count))]
    slice x6 -> x0, local copies, waits for them, and re-layouts: 15.4 us -> none  [solve(): rows[part]]
    dot_general x8, matrix products: 17.3 us -> 29.1 us  [the longest x4 16.3 us: solve(): jnp.einsum('mrj,mjn->mrn', rows, recv_tables[shift], preferred_element_ty...]
    another operation x6 -> x2, local copies, waits for them, and re-layouts: 10.7 us -> 0.17 us  [the longest x4 10.5 us: bands_of(): jnp.stack(parts).reshape(lat_count, width, level_count, row_count)]
    unnamed x27 -> x43, local copies, waits for them, and re-layouts: 6.02 us -> 14.9 us
  transfers between devices with their start and end apart: 3 -> 5, of which waited for: 2 -> 4; matrix products, arithmetic and copies ran while one was open for 1% -> 13% of each run, Pallas kernels for 0% -> 0%
where the time goes in v2:
time: 328 us; the launch traced here: 326 us
  blocking collectives  88 us (27%)
  waiting for transfers between devices  81.5 us (25%)
  local copies, waits for them, and re-layouts  63.9 us (19%)
  matrix products  46.7 us (14%)
  Pallas kernels  24.8 us (8%)
  starting transfers between devices  13.7 us (4%)
  other arithmetic  6.86 us (2%)
    ppermute x4, waiting for transfers between devices, send(): return lax.ppermute(array, 'lat', pairs)  81.5 us
    all_to_all x1, blocking collectives, clone(): lax.all_to_all(chosen, 'traj', split_axis=0, concat_axis=0, tiled=True)  46.4 us
    unnamed x1, blocking collectives  41.5 us
    pallas_call x3, Pallas kernels, row_call(): pl.pallas_call(kernel, grid=(rows // block,), in_specs=specs, out_specs=[...  24.8 us
    dot_general x4, matrix products, solve(): jnp.einsum('mrj,mjn->mrn', rows, recv_tables[shift], preferred_element_ty...  16.3 us
    optimization_barrier x4, local copies, waits for them, and re-layouts, bands_of(): part = lax.optimization_barrier(part.reshape(width, level_count, row_count))  15.2 us
    convert_element_type x4, local copies, waits for them, and re-layouts, bands_of(): part = jnp.einsum('mrn,mjn->mrj', rows, send_tables[shift], preferred_ele...  15 us
    optimization_barrier x4, local copies, waits for them, and re-layouts, solve(): rows = lax.optimization_barrier(arrived.transpose(2, 0, 1))  14.9 us
  transfers between devices with their start and end apart: 5, of which 4 were waited for; matrix products, arithmetic and copies ran while one was open for 13% of the time, Pallas kernels for 0%

profile of v2, /device:TPU:0, one launch (start us, length us, event | category | flops | bytes accessed | tf_op | source)
XLA Modules:
  0.0 326.4 jit_solution(2144497190404278619)
XLA Ops:
  0.9 1.7 select_convert_fusion
  2.6 2.0 fusion.28.mixer_ref
  4.8 3.4 %copy-done.1 = f32[1,56,96,384]{3,2,1,0:T(8,128)S(1)} copy-done((f32[1,56,96,384]{3,2,1,0:T(8,128)S(1)}, f32[1,56,96,384]{3,2,1,0:T(8,128)}, u32[]{:S(2)}) %copy-start.1) | copy-done | bytes 8257560
  9.1 7.6 %shard_map.82 = (bf16[56,96,128]{2,1,0:T(8,128)(2,1)S(1)}, bf16[56,96,128]{2,1,0:T(8,128)(2,1)}) custom-call(f32[56,96,384]{2,1,0:T(8,128)S(1)} %bitcast.127, bf16[448,448]{1,0:T(8,128)(2,1)S(1)} %copy-done.4, f32[96,128]{1,0:T(8,128)S(1)} %broadcast_in_dim.65.scale_ref, bf16[384,256]{1,0:T(8,128)(2,1)S(1)} %pad_maximum_fusion.1.forward_ref), custom_call_target="tpu_custom_call" | custom-call | tf_op jit(solution)/shard_map/pallas_call | solution.py:146
  17.8 3.0 collective-permute-start
  20.7 3.7 %copy.37 = bf16[128,56,96]{2,1,0:T(8,128)(2,1)} copy(bf16[128,56,96]{0,2,1:T(8,128)(2,1)} %bitcast.130) | data formatting | bytes 2752512 | tf_op jit(solution)/shard_map/optimization_barrier | solution.py:249
  24.6 4.5 %fusion.22 = f32[64,112,128]{2,1,0:T(8,128)} fusion(bf16[64,112,96]{2,1,0:T(8,128)(2,1)} %bitcast.138, bf16[64,2,96,128]{3,2,1,0:T(8,128)(2,1)S(1)} %bitcast.120, s32[]{:T(128)S(6)} %select_n.206), kind=kOutput, calls=%fused_computation.26 | convolution fusion | flops 176160768 | bytes 6619140 | tf_op jit(solution)/shard_map/mrj,mjn->mrn/dot_general | solution.py:251
  29.0 22.2 %collective-permute-done = bf16[56,96,128]{2,1,0:T(8,128)(2,1)} collective-permute-done((bf16[56,96,128]{2,1,0:T(8,128)(2,1)}, bf16[56,96,128]{2,1,0:T(8,128)(2,1)}, u32[]{:S(2)}, u32[]{:S(2)}) %collective-permute-start) | collective-permute-done | bytes 1376288 | tf_op jit(solution)/shard_map/ppermute | solution.py:243
  51.2 3.7 %copy.40 = bf16[128,56,96]{2,1,0:T(8,128)(2,1)} copy(bf16[128,56,96]{0,2,1:T(8,128)(2,1)} %bitcast.12) | data formatting | bytes 2752512 | tf_op jit(solution)/shard_map/optimization_barrier | solution.py:249
  55.0 3.7 %convolution_add_fusion.1 = f32[64,112,128]{2,1,0:T(8,128)S(1)} fusion(f32[64,112,128]{2,1,0:T(8,128)} %fusion.22, bf16[64,112,96]{2,1,0:T(8,128)(2,1)} %bitcast.144, bf16[64,2,96,128]{3,2,1,0:T(8,128)(2,1)S(1)} %bitcast.121, s32[]{:T(128)S(6)} %select_n.208), kind=kOutput, calls=%fused_computation.8 | convolution fusion | flops 177078272 | bytes 10289156 | tf_op jit(solution)/shard_map/mrj,mjn->mrn/dot_general | solution.py:251
  58.7 3.6 %fusion.49 = f32[128,128,56]{1,2,0:T(8,128)S(1)} fusion(f32[128,56,128]{2,1,0:T(8,128)S(1)} %bitcast.134, f32[56,56]{1,0:T(8,128)S(1)} %copy-done.12), kind=kOutput, calls=%fused_computation.67 | convolution fusion | flops 616562688 | bytes 7352576 | tf_op jit(solution)/shard_map/kl,pmln->pmkn/dot_general | solution.py:60
  62.4 4.7 %fusion.8 = bf16[128,128,56]{1,2,0:T(8,128)(2,1)} fusion(f32[128,128,56]{1,2,0:T(8,128)S(1)} %fusion.49, f32[56,128]{1,0:T(8,128)S(1)} %multiply_add_fusion, f32[56,56]{1,0:T(8,128)S(1)} %copy-done.17), kind=kOutput, calls=%fused_computation.12 | convolution fusion | flops 618397696 | bytes 5546240 | tf_op jit(solution)/shard_map/lk,pmkn->pmln/dot_general | solution.py:63
  67.0 6.3 %all-to-all-start = ((bf16[16,448,128]{2,1,0:T(8,128)(2,1)}), bf16[16,448,128]{2,1,0:T(8,128)(2,1)}, u32[]{:S(2)}, u32[]{:S(2)}) async-start(bf16[16,448,128]{2,1,0:T(8,128)(2,1)} %bitcast.146), calls=%async_computation | async-start | bytes 3670016 | tf_op jit(solution)/shard_map/all_to_all | solution.py:197
  75.4 41.5 %all-reduce = s32[16]{0:T(128)S(1)} all-reduce(s32[16]{0:T(128)S(1)} %dynamic-update-slice), channel_id=1, replica_groups=mesh['traj'=16,'lat'=2] {'traj'}, use_global_device_ids=true, to_apply=%add | all-reduce | flops 16 | bytes 128
  117.7 3.5 %gather_fusion = bf16[16,448,128]{2,1,0:T(8,128)(2,1)} fusion(bf16[16,448,128]{2,1,0:T(8,128)(2,1)} %all-to-all-done, s32[1024]{0:T(1024)S(1)} %pad_clamp_fusion), kind=kCustom, calls=%fused_computation | custom fusion | bytes 3670080 | tf_op jit(solution)/shard_map/jit(_take)/gather | solution.py:198
  121.2 1.7 broadcast_select_fusion
  122.9 46.4 %all_to_all.10 = bf16[16,448,128]{2,1,0:T(8,128)(2,1)S(1)} all-to-all(bf16[16,448,128]{2,1,0:T(8,128)(2,1)S(1)} %broadcast_select_fusion), channel_id=1, replica_groups=mesh['traj'=16,'lat'=2] {'traj'}, dimensions={0} | all-to-all | bytes 3670016 | tf_op jit(solution)/shard_map/all_to_all | solution.py:199
  169.4 1.2 copy-done.10
  170.6 2.5 convolution_convert_fusion.2
  173.0 3.8 %copy.46 = bf16[64,112,96]{2,1,0:T(8,128)(2,1)} copy(bf16[64,112,96]{1,2,0:T(8,128)(2,1)} %convolution_convert_fusion.2) | data formatting | bytes 2752512 | tf_op jit(solution)/shard_map/convert_element_type | solution.py:263
  176.8 3.8 %copy.47 = bf16[128,56,96]{0,2,1:T(8,128)(2,1)} copy(bf16[128,56,96]{2,1,0:T(8,128)(2,1)} %bitcast.140) | data formatting | bytes 2752512 | tf_op jit(solution)/shard_map/optimization_barrier | solution.py:264
  180.6 1.5 collective-permute-start.1
  182.1 1.9 multiply_convert_fusion
  184.1 4.0 %convolution_convert_fusion.3 = bf16[64,112,96]{1,2,0:T(8,128)(2,1)} fusion(bf16[64,112,128]{2,1,0:T(8,128)(2,1)} %bitcast.133, bf16[64,2,96,128]{3,2,1,0:T(8,128)(2,1)S(1)} %bitcast.119, s32[]{:T(128)S(6)} %select_n.215), kind=kOutput, calls=%fused_computation.17 | convolution fusion | flops 176848896 | bytes 4784132 | tf_op jit(solution)/shard_map/mrn,mjn->mrj/dot_general | solution.py:261
  188.1 3.8 %copy.44 = bf16[64,112,96]{2,1,0:T(8,128)(2,1)} copy(bf16[64,112,96]{1,2,0:T(8,128)(2,1)} %convolution_convert_fusion.3) | data formatting | bytes 2752512 | tf_op jit(solution)/shard_map/convert_element_type | solution.py:263
  191.8 3.8 %copy.45 = bf16[128,56,96]{0,2,1:T(8,128)(2,1)} copy(bf16[128,56,96]{2,1,0:T(8,128)(2,1)} %bitcast.141) | data formatting | bytes 2752512 | tf_op jit(solution)/shard_map/optimization_barrier | solution.py:264
  195.6 18.2 %collective-permute-done.1.refs_1_ = bf16[56,96,128]{2,1,0:T(8,128)(2,1)} collective-permute-done((bf16[56,96,128]{2,1,0:T(8,128)(2,1)}, bf16[56,96,128]{2,1,0:T(8,128)(2,1)}, u32[]{:S(2)}, u32[]{:S(2)}) %collective-permute-start.1) | collective-permute-done | bytes 1376288 | tf_op jit(solution)/shard_map/ppermute | solution.py:243
  213.8 1.3 copy-done.2
  216.9 10.1 %shard_map.83 = (bf16[56,96,128]{2,1,0:T(8,128)(2,1)S(1)}, bf16[56,96,128]{2,1,0:T(8,128)(2,1)}) custom-call(bf16[256,384]{1,0:T(8,128)(2,1)S(1)} %pad_maximum_fusion.backward_ref, bf16[448,448]{1,0:T(8,128)(2,1)S(1)} %copy-done.5, f32[96,128]{1,0:T(8,128)S(1)} %copy-done.9, bf16[384,256]{1,0:T(8,128)(2,1)S(1)} %pad_maximum_fusion.1.forward_ref, ...), custom_call_target="tpu_custom_call" | custom-call | tf_op jit(solution)/shard_map/pallas_call | solution.py:146
  228.2 1.5 collective-permute-start.2
  229.6 3.7 %copy.48 = bf16[128,56,96]{2,1,0:T(8,128)(2,1)} copy(bf16[128,56,96]{0,2,1:T(8,128)(2,1)} %bitcast.131) | data formatting | bytes 2752512 | tf_op jit(solution)/shard_map/optimization_barrier | solution.py:249
  233.4 4.4 %fusion.20 = f32[64,112,128]{2,1,0:T(8,128)} fusion(bf16[64,112,96]{2,1,0:T(8,128)(2,1)} %bitcast.139, bf16[64,2,96,128]{3,2,1,0:T(8,128)(2,1)S(1)} %bitcast.123, s32[]{:T(128)S(6)} %select_n.206), kind=kOutput, calls=%fused_computation.24 | convolution fusion | flops 176160768 | bytes 6619140 | tf_op jit(solution)/shard_map/mrj,mjn->mrn/dot_general | solution.py:251
  237.8 22.6 %collective-permute-done.2 = bf16[56,96,128]{2,1,0:T(8,128)(2,1)} collective-permute-done((bf16[56,96,128]{2,1,0:T(8,128)(2,1)}, bf16[56,96,128]{2,1,0:T(8,128)(2,1)}, u32[]{:S(2)}, u32[]{:S(2)}) %collective-permute-start.2) | collective-permute-done | bytes 1376288 | tf_op jit(solution)/shard_map/ppermute | solution.py:243
  260.5 3.7 %copy.50 = bf16[128,56,96]{2,1,0:T(8,128)(2,1)} copy(bf16[128,56,96]{0,2,1:T(8,128)(2,1)} %bitcast.32) | data formatting | bytes 2752512 | tf_op jit(solution)/shard_map/optimization_barrier | solution.py:249
  264.2 3.7 %convolution_add_fusion = f32[64,112,128]{2,1,0:T(8,128)S(1)} fusion(f32[64,112,128]{2,1,0:T(8,128)} %fusion.20, bf16[64,112,96]{2,1,0:T(8,128)(2,1)} %bitcast.145, bf16[64,2,96,128]{3,2,1,0:T(8,128)(2,1)S(1)} %bitcast.125, s32[]{:T(128)S(6)} %select_n.208), kind=kOutput, calls=%fused_computation.7 | convolution fusion | flops 177078272 | bytes 10289156 | tf_op jit(solution)/shard_map/mrj,mjn->mrn/dot_general | solution.py:251
  267.9 3.6 %fusion.47 = f32[128,128,56]{1,2,0:T(8,128)S(1)} fusion(f32[128,56,128]{2,1,0:T(8,128)S(1)} %bitcast.135, f32[56,56]{1,0:T(8,128)S(1)} %copy-done.13), kind=kOutput, calls=%fused_computation.65 | convolution fusion | flops 616562688 | bytes 7352576 | tf_op jit(solution)/shard_map/kl,pmln->pmkn/dot_general | solution.py:60
  271.6 3.6 %fusion.11 = bf16[128,128,56]{1,2,0:T(8,128)(2,1)S(1)} fusion(f32[128,128,56]{1,2,0:T(8,128)S(1)} %fusion.47, f32[56,128]{1,0:T(8,128)S(1)} %copy-done.15, f32[56,56]{1,0:T(8,128)S(1)} %copy-done.18), kind=kOutput, calls=%fused_computation.13 | convolution fusion | flops 618397696 | bytes 5546240 | tf_op jit(solution)/shard_map/lk,pmkn->pmln/dot_general | solution.py:63
  275.2 1.2 copy-done.11
  276.5 2.4 convolution_convert_fusion
  278.9 3.8 %copy.54 = bf16[64,112,96]{2,1,0:T(8,128)(2,1)} copy(bf16[64,112,96]{1,2,0:T(8,128)(2,1)} %convolution_convert_fusion) | data formatting | bytes 2752512 | tf_op jit(solution)/shard_map/convert_element_type | solution.py:263
  282.7 3.8 %copy.55 = bf16[128,56,96]{0,2,1:T(8,128)(2,1)} copy(bf16[128,56,96]{2,1,0:T(8,128)(2,1)} %bitcast.142) | data formatting | bytes 2752512 | tf_op jit(solution)/shard_map/optimization_barrier | solution.py:264
  286.5 1.5 collective-permute-start.3
  287.9 3.9 %convolution_convert_fusion.1 = bf16[64,112,96]{1,2,0:T(8,128)(2,1)} fusion(bf16[64,112,128]{2,1,0:T(8,128)(2,1)} %bitcast.137, bf16[64,2,96,128]{3,2,1,0:T(8,128)(2,1)S(1)} %bitcast.122, s32[]{:T(128)S(6)} %select_n.215), kind=kOutput, calls=%fused_computation.15 | convolution fusion | flops 176848896 | bytes 4784132 | tf_op jit(solution)/shard_map/mrn,mjn->mrj/dot_general | solution.py:261
  291.9 3.8 %copy.52 = bf16[64,112,96]{2,1,0:T(8,128)(2,1)} copy(bf16[64,112,96]{1,2,0:T(8,128)(2,1)} %convolution_convert_fusion.1) | data formatting | bytes 2752512 | tf_op jit(solution)/shard_map/convert_element_type | solution.py:263
  295.6 3.8 %copy.53 = bf16[128,56,96]{0,2,1:T(8,128)(2,1)} copy(bf16[128,56,96]{2,1,0:T(8,128)(2,1)} %bitcast.143) | data formatting | bytes 2752512 | tf_op jit(solution)/shard_map/optimization_barrier | solution.py:264
  299.4 18.5 %collective-permute-done.3.refs_1_ = bf16[56,96,128]{2,1,0:T(8,128)(2,1)} collective-permute-done((bf16[56,96,128]{2,1,0:T(8,128)(2,1)}, bf16[56,96,128]{2,1,0:T(8,128)(2,1)}, u32[]{:S(2)}, u32[]{:S(2)}) %collective-permute-start.3) | collective-permute-done | bytes 1376288 | tf_op jit(solution)/shard_map/ppermute | solution.py:243
  317.9 1.3 copy-done.3
  319.3 7.1 %shard_map.84 = f32[56,96,384]{2,1,0:T(8,128)} custom-call(bf16[256,384]{1,0:T(8,128)(2,1)S(1)} %pad_maximum_fusion.backward_ref, bf16[56,96,128]{2,1,0:T(8,128)(2,1)S(1)} %bitcast.129, bf16[56,96,128]{2,1,0:T(8,128)(2,1)} %collective-permute-done.3.refs_1_), custom_call_target="tpu_custom_call" | custom-call | tf_op jit(solution)/shard_map/pallas_call | solution.py:146
  (62 shorter events, 8.3 us)
Async XLA Ops:
  0.0 24.6 %copy-start = (bf16[64,192,128]{2,1,0:T(8,128)(2,1)S(1)}, bf16[64,192,128]{2,1,0:T(8,128)(2,1)}, u32[]{:S(2)}) copy-start(bf16[64,192,128]{2,1,0:T(8,128)(2,1)} %param.12) | copy-start | bytes 9437188
  4.8 3.4 %copy-start.1 = (f32[1,56,96,384]{3,2,1,0:T(8,128)S(1)}, f32[1,56,96,384]{3,2,1,0:T(8,128)}, u32[]{:S(2)}) copy-start(f32[1,56,96,384]{3,2,1,0:T(8,128)} %param.8) | copy-start | bytes 24772612
  8.1 1.0 copy-start.4
  9.1 7.6 %copy-start.8 = (f32[96,128]{1,0:T(8,128)}, f32[96,128]{1,0:T(8,128)S(1)}, u32[]{:S(2)}) copy-start(f32[96,128]{1,0:T(8,128)S(1)} %broadcast_in_dim.65.scale_ref) | copy-start | bytes 147460
  16.7 1.1 copy-start.6
  17.8 6.7 %copy-start.16 = (f32[56]{0:T(128)S(1)}, f32[56]{0:T(128)}, u32[]{:S(2)}) copy-start(f32[56]{0:T(128)} %param.15) | copy-start | bytes 676
  17.8 33.5 %collective-permute-start = (bf16[56,96,128]{2,1,0:T(8,128)(2,1)}, bf16[56,96,128]{2,1,0:T(8,128)(2,1)}, u32[]{:S(2)}, u32[]{:S(2)}) collective-permute-start(bf16[56,96,128]{2,1,0:T(8,128)(2,1)} %get-tuple-element.10), channel_id=1, source_target_pairs={{0,1},{1,0},{2,3},{3,2},{4,5},{5,4},{6,7},{7,6},{8,9},{9,8},{10,11... | collective-permute-start | bytes 4128776 | tf_op jit(solution)/shard_map/ppermute | solution.py:243
  24.6 37.8 %copy-start.14 = (f32[56,128]{1,0:T(8,128)}, f32[56,128]{1,0:T(8,128)S(1)}, u32[]{:S(2)}) copy-start(f32[56,128]{1,0:T(8,128)S(1)} %multiply_add_fusion) | copy-start | bytes 86020
  55.0 3.7 %copy-start.12 = (f32[56,56]{1,0:T(8,128)S(1)}, f32[56,56]{1,0:T(8,128)}, u32[]{:S(2)}) copy-start(f32[56,56]{1,0:T(8,128)} %param.13) | copy-start | bytes 37636
  58.7 3.7 %copy-start.17 = (f32[56,56]{1,0:T(8,128)S(1)}, f32[56,56]{1,0:T(8,128)}, u32[]{:S(2)}) copy-start(f32[56,56]{1,0:T(8,128)} %param.14) | copy-start | bytes 37636
  67.0 7.0 %copy-start.19 = (u32[32]{0:T(128)S(1)}, u32[32]{0:T(128)}, u32[]{:S(2)}) copy-start(u32[32]{0:T(128)} %constant.209) | copy-start | bytes 388
  67.0 50.6 %all-to-all-start = ((bf16[16,448,128]{2,1,0:T(8,128)(2,1)}), bf16[16,448,128]{2,1,0:T(8,128)(2,1)}, u32[]{:S(2)}, u32[]{:S(2)}) async-start(bf16[16,448,128]{2,1,0:T(8,128)(2,1)} %bitcast.146), calls=%async_computation | async-start | bytes 3670016 | tf_op jit(solution)/shard_map/all_to_all | solution.py:197
  169.4 1.2 copy-start.10
  180.6 33.2 %collective-permute-start.1 = (bf16[56,96,128]{2,1,0:T(8,128)(2,1)}, bf16[56,96,128]{2,1,0:T(8,128)(2,1)}, u32[]{:S(2)}, u32[]{:S(2)}) collective-permute-start(bf16[56,96,128]{2,1,0:T(8,128)(2,1)} %bitcast.147), channel_id=1, source_target_pairs={{0,1},{1,0},{2,3},{3,2},{4,5},{5,4},{6,7},{7,6},{8,9},{9,8},{10,11... | collective-permute-start | bytes 4128776 | tf_op jit(solution)/shard_map/ppermute | solution.py:243
  213.8 1.3 copy-start.2
  215.1 1.0 copy-start.5
  216.2 0.8 copy-start.9
  227.1 1.1 copy-start.7
  228.2 32.3 %collective-permute-start.2 = (bf16[56,96,128]{2,1,0:T(8,128)(2,1)}, bf16[56,96,128]{2,1,0:T(8,128)(2,1)}, u32[]{:S(2)}, u32[]{:S(2)}) collective-permute-start(bf16[56,96,128]{2,1,0:T(8,128)(2,1)} %get-tuple-element.12), channel_id=1, source_target_pairs={{0,1},{1,0},{2,3},{3,2},{4,5},{5,4},{6,7},{7,6},{8,9},{9,8},{10,11... | collective-permute-start | bytes 4128776 | tf_op jit(solution)/shard_map/ppermute | solution.py:243
  264.2 3.7 %copy-start.13 = (f32[56,56]{1,0:T(8,128)S(1)}, f32[56,56]{1,0:T(8,128)}, u32[]{:S(2)}) copy-start(f32[56,56]{1,0:T(8,128)} %param.13) | copy-start | bytes 37636
  267.9 3.7 %copy-start.15 = (f32[56,128]{1,0:T(8,128)S(1)}, f32[56,128]{1,0:T(8,128)}, u32[]{:S(2)}) copy-start(f32[56,128]{1,0:T(8,128)} %copy-done.14) | copy-start | bytes 86020
  267.9 3.7 %copy-start.18 = (f32[56,56]{1,0:T(8,128)S(1)}, f32[56,56]{1,0:T(8,128)}, u32[]{:S(2)}) copy-start(f32[56,56]{1,0:T(8,128)} %param.14) | copy-start | bytes 37636
  275.2 1.2 copy-start.11
  286.5 31.5 %collective-permute-start.3 = (bf16[56,96,128]{2,1,0:T(8,128)(2,1)}, bf16[56,96,128]{2,1,0:T(8,128)(2,1)}, u32[]{:S(2)}, u32[]{:S(2)}) collective-permute-start(bf16[56,96,128]{2,1,0:T(8,128)(2,1)} %bitcast.148), channel_id=1, source_target_pairs={{0,1},{1,0},{2,3},{3,2},{4,5},{5,4},{6,7},{7,6},{8,9},{9,8},{10,11... | collective-permute-start | bytes 4128776 | tf_op jit(solution)/shard_map/ppermute | solution.py:243
  317.9 1.3 copy-start.3

commit v3 on v2

--- a/solution.py
+++ b/solution.py
@@ -126,6 +126,33 @@
 
 def last_kernel(backward_ref, *refs):
     refs[-1][...] = from_bands(refs[:-1], backward_ref[...])
+
+
+def bands_kernel(rows_ref, table_ref, out_ref):
+    for at in range(rows_ref.shape[0]):
+        out_ref[at] = lax.dot_general(
+            rows_ref[at],
+            table_ref[at],
+            (((1,), (1,)), ((), ())),
+            preferred_element_type=jnp.float32,
+        ).astype(jnp.bfloat16)
+
+
+def wave_bands(rows, table):
+    shape = (rows.shape[0], rows.shape[1], table.shape[1])
+    return pl.pallas_call(
+        bands_kernel,
+        grid=(shape[0] // 16,),
+        in_specs=[by_rows(rows.shape, 0, 16), by_rows(table.shape, 0, 16)],
+        out_specs=by_rows(shape, 0, 16),
+        out_shape=jax.ShapeDtypeStruct(shape, jnp.bfloat16),
+        cost_estimate=pl.CostEstimate(
+            flops=2 * math.prod(shape) * rows.shape[2],
+            bytes_accessed=2 * (rows.size + table.size + math.prod(shape)),
+            transcendentals=0,
+        ),
+        compiler_params=pltpu.CompilerParams(vmem_limit_bytes=32 * 1024 * 1024),
+    )(rows, table)
 
 
 def fixed(array):
@@ -258,9 +285,7 @@
         rows = implicit.reshape(local_waves, 2 * level_count, degree_count)
         result = []
         for shift in shifts:
-            part = jnp.einsum(
-                "mrn,mjn->mrj", rows, send_tables[shift], preferred_element_type=jnp.float32
-            ).astype(jnp.bfloat16)
+            part = wave_bands(rows, send_tables[shift])
             part = lax.optimization_barrier(part.reshape(width, level_count, row_count))
             result.append(send(part.transpose(1, 2, 0), shift))
         return result

time: 328 us -> 308 us (0.939)
  local copies, waits for them, and re-layouts: 63.9 us -> 46.7 us
  matrix products: 46.7 us -> 30 us
  waiting for transfers between devices: 81.5 us -> 89.1 us
  Pallas kernels: 24.8 us -> 30.7 us
    convert_element_type x4 -> x0, local copies, waits for them, and re-layouts: 15 us -> none  [bands_of(): part = jnp.einsum('mrn,mjn->mrj', rows, send_tables[shift], preferred_ele...]
    dot_general x4 -> x0, matrix products: 12.8 us -> none  [bands_of(): jnp.einsum('mrn,mjn->mrj', rows, send_tables[shift], preferred_element_ty...]
    ppermute x4, waiting for transfers between devices: 81.5 us -> 89.1 us  [send(): return lax.ppermute(array, 'lat', pairs)]
    pallas_call x0 -> x4, Pallas kernels: none -> 6.34 us  [wave_bands(): pl.pallas_call(bands_kernel, grid=(shape[0] // 16,), in_specs=[by_rows(ro...]
    squeeze x2 -> x3, local copies, waits for them, and re-layouts: 0.05 us -> 3.48 us  [take(): lax.dynamic_index_in_dim(array, part % lat_count, axis, keepdims=False)]
    unnamed x43 -> x45, local copies, waits for them, and re-layouts: 14.9 us -> 14.4 us
  transfers between devices with their start and end apart: 5 -> 5, of which waited for: 4 -> 4; matrix products, arithmetic and copies ran while one was open for 13% -> 9% of each run, Pallas kernels for 0% -> 1%
where the time goes in v3:
time: 308 us; the launch traced here: 307 us
  waiting for transfers between devices  89.1 us (29%)
  blocking collectives  87.8 us (29%)
  local copies, waits for them, and re-layouts  46.7 us (15%)
  Pallas kernels  30.7 us (10%)
  matrix products  30 us (10%)
  starting transfers between devices  13.8 us (4%)
  other arithmetic  7.39 us (2%)
    ppermute x4, waiting for transfers between devices, send(): return lax.ppermute(array, 'lat', pairs)  89.1 us
    all_to_all x1, blocking collectives, clone(): lax.all_to_all(chosen, 'traj', split_axis=0, concat_axis=0, tiled=True)  46.3 us
    unnamed x1, blocking collectives  41.6 us
    pallas_call x3, Pallas kernels, row_call(): pl.pallas_call(kernel, grid=(rows // block,), in_specs=specs, out_specs=[...  24.4 us
    optimization_barrier x4, local copies, waits for them, and re-layouts, bands_of(): part = lax.optimization_barrier(part.reshape(width, level_count, row_count))  14.6 us
    unnamed x45, local copies, waits for them, and re-layouts  14.4 us
    dot_general x4, matrix products, solve(): jnp.einsum('mrj,mjn->mrn', rows, recv_tables[shift], preferred_element_ty...  13.6 us
    optimization_barrier x4, local copies, waits for them, and re-layouts, solve(): rows = lax.optimization_barrier(arrived.transpose(2, 0, 1))  11.9 us
  transfers between devices with their start and end apart: 5, of which 4 were waited for; matrix products, arithmetic and copies ran while one was open for 9% of the time, Pallas kernels for 1%

profile of v3, /device:TPU:0, one launch (start us, length us, event | category | flops | bytes accessed | tf_op | source)
XLA Modules:
  0.0 306.6 jit_solution(18216021433047099950)
XLA Ops:
  0.7 1.7 select_convert_fusion
  2.5 1.3 fusion.20.mixer_ref
  3.9 3.4 %copy-done.3 = f32[1,56,96,384]{3,2,1,0:T(8,128)S(1)} copy-done((f32[1,56,96,384]{3,2,1,0:T(8,128)S(1)}, f32[1,56,96,384]{3,2,1,0:T(8,128)}, u32[]{:S(2)}) %copy-start.3) | copy-done | bytes 8257560
  7.3 7.1 %shard_map.82 = (bf16[56,96,128]{2,1,0:T(8,128)(2,1)S(1)}, bf16[56,96,128]{2,1,0:T(8,128)(2,1)S(1)}) custom-call(f32[56,96,384]{2,1,0:T(8,128)S(1)} %bitcast.109, bf16[448,448]{1,0:T(8,128)(2,1)S(1)} %fusion.20.mixer_ref, f32[96,128]{1,0:T(8,128)S(1)} %broadcast_in_dim.65.scale_ref, bf16[384,256]{1,0:T(8,128)(2,1)S(1)} %pad_maximum_fusion.1.forward_ref), custom_call_target="tpu_custom_call" | custom-call | tf_op jit(solution)/shard_map/pallas_call | solution.py:173
  14.4 3.0 collective-permute-start
  17.4 2.9 copy.33
  20.4 3.4 %dynamic-slice_bitcast_fusion = (bf16[64,96,128]{2,1,0:T(8,128)(2,1)}, bf16[64,96,128]{2,1,0:T(8,128)(2,1)S(1)}) fusion(bf16[64,2,96,128]{3,2,1,0:T(8,128)(2,1)} %bitcast.122, s32[]{:T(128)S(6)} %select_n.215, s32[]{:T(128)S(6)} %select_n.208), kind=kLoop, calls=%fused_computation.18 | loop fusion | bytes 6291464 | tf_op jit(solution)/shard_map/jit(dynamic_index_in_dim)/squeeze | solution.py:255
  24.2 2.9 fusion.16
  27.1 20.6 %collective-permute-done = bf16[56,96,128]{2,1,0:T(8,128)(2,1)} collective-permute-done((bf16[56,96,128]{2,1,0:T(8,128)(2,1)S(1)}, bf16[56,96,128]{2,1,0:T(8,128)(2,1)}, u32[]{:S(2)}, u32[]{:S(2)}) %collective-permute-start) | collective-permute-done | bytes 1376288 | tf_op jit(solution)/shard_map/ppermute | solution.py:270
  47.7 2.9 copy.36
  50.7 3.2 %convolution_add_fusion.1 = f32[64,112,128]{2,1,0:T(8,128)S(1)} fusion(f32[64,112,128]{2,1,0:T(8,128)} %fusion.16, bf16[64,112,96]{2,1,0:T(8,128)(2,1)S(1)} %bitcast.127, bf16[64,96,128]{2,1,0:T(8,128)(2,1)S(1)} %get-tuple-element.16.table_ref), kind=kOutput, calls=%fused_computation.8 | convolution fusion | flops 177078272 | bytes 10289152 | tf_op jit(solution)/shard_map/mrj,mjn->mrn/dot_general | solution.py:278
  53.9 3.4 %fusion.37 = f32[128,128,56]{1,2,0:T(8,128)S(1)} fusion(f32[128,56,128]{2,1,0:T(8,128)S(1)} %bitcast.120, f32[56,56]{1,0:T(8,128)S(1)} %copy-done), kind=kOutput, calls=%fused_computation.53 | convolution fusion | flops 616562688 | bytes 7352576 | tf_op jit(solution)/shard_map/kl,pmln->pmkn/dot_general | solution.py:60
  57.3 4.7 %fusion.8 = bf16[128,128,56]{1,2,0:T(8,128)(2,1)} fusion(f32[128,128,56]{1,2,0:T(8,128)S(1)} %fusion.37, f32[56,128]{1,0:T(8,128)S(1)} %multiply_add_fusion, f32[56,56]{1,0:T(8,128)S(1)} %copy-done.18), kind=kOutput, calls=%fused_computation.12 | convolution fusion | flops 618397696 | bytes 5546240 | tf_op jit(solution)/shard_map/lk,pmkn->pmln/dot_general | solution.py:63
  62.0 6.3 %all-to-all-start = ((bf16[16,448,128]{2,1,0:T(8,128)(2,1)}), bf16[16,448,128]{2,1,0:T(8,128)(2,1)S(1)}, u32[]{:S(2)}, u32[]{:S(2)}) async-start(bf16[16,448,128]{2,1,0:T(8,128)(2,1)} %bitcast.129), calls=%async_computation | async-start | bytes 3670016 | tf_op jit(solution)/shard_map/all_to_all | solution.py:224
  70.3 41.6 %all-reduce = s32[16]{0:T(128)S(1)} all-reduce(s32[16]{0:T(128)S(1)} %dynamic-update-slice), channel_id=1, replica_groups=mesh['traj'=16,'lat'=2] {'traj'}, use_global_device_ids=true, to_apply=%add | all-reduce | flops 16 | bytes 128
  112.6 2.0 gather_fusion
  114.6 1.7 broadcast_select_fusion
  116.3 46.3 %all_to_all.10 = bf16[16,448,128]{2,1,0:T(8,128)(2,1)S(1)} all-to-all(bf16[16,448,128]{2,1,0:T(8,128)(2,1)S(1)} %broadcast_select_fusion), channel_id=1, replica_groups=mesh['traj'=16,'lat'=2] {'traj'}, dimensions={0} | all-to-all | bytes 3670016 | tf_op jit(solution)/shard_map/all_to_all | solution.py:226
  162.6 1.6 shard_map.84
  164.2 1.2 copy-done.7
  165.4 3.8 %copy.41 = bf16[128,56,96]{0,2,1:T(8,128)(2,1)} copy(bf16[128,56,96]{2,1,0:T(8,128)(2,1)} %bitcast.115) | data formatting | bytes 2752512 | tf_op jit(solution)/shard_map/optimization_barrier | solution.py:289
  169.2 1.5 collective-permute-start.1
  170.7 1.9 multiply_convert_fusion
  173.4 1.4 copy-done.1
  174.8 1.6 shard_map.83
  176.4 1.2 copy-done.5
  177.6 3.5 %copy.40 = bf16[128,56,96]{0,2,1:T(8,128)(2,1)S(1)} copy(bf16[128,56,96]{2,1,0:T(8,128)(2,1)} %bitcast.113) | data formatting | bytes 2752512 | tf_op jit(solution)/shard_map/optimization_barrier | solution.py:289
  181.1 21.3 %collective-permute-done.1.refs_1_ = bf16[56,96,128]{2,1,0:T(8,128)(2,1)} collective-permute-done((bf16[56,96,128]{2,1,0:T(8,128)(2,1)}, bf16[56,96,128]{2,1,0:T(8,128)(2,1)}, u32[]{:S(2)}, u32[]{:S(2)}) %collective-permute-start.1) | collective-permute-done | bytes 1376288 | tf_op jit(solution)/shard_map/ppermute | solution.py:270
  202.4 0.9 copy-done.11
  204.2 10.2 %shard_map.85 = (bf16[56,96,128]{2,1,0:T(8,128)(2,1)S(1)}, bf16[56,96,128]{2,1,0:T(8,128)(2,1)}) custom-call(bf16[256,384]{1,0:T(8,128)(2,1)S(1)} %copy-done.12, bf16[448,448]{1,0:T(8,128)(2,1)S(1)} %copy-done.9, f32[96,128]{1,0:T(8,128)S(1)} %broadcast_in_dim.65.scale_ref, bf16[384,256]{1,0:T(8,128)(2,1)S(1)} %copy-done.11, ...), custom_call_target="tpu_custom_call" | custom-call | tf_op jit(solution)/shard_map/pallas_call | solution.py:173
  214.5 1.1 copy-done.14
  215.5 1.5 collective-permute-start.2
  217.1 2.9 copy.42
  220.0 4.4 %fusion.14 = f32[64,112,128]{2,1,0:T(8,128)} fusion(bf16[64,112,96]{2,1,0:T(8,128)(2,1)S(1)} %bitcast.126, bf16[64,2,96,128]{3,2,1,0:T(8,128)(2,1)} %bitcast.123, s32[]{:T(128)S(6)} %select_n.206), kind=kOutput, calls=%fused_computation.14 | convolution fusion | flops 176160768 | bytes 6619140 | tf_op jit(solution)/shard_map/mrj,mjn->mrn/dot_general | solution.py:278
  224.4 23.5 %collective-permute-done.2 = bf16[56,96,128]{2,1,0:T(8,128)(2,1)} collective-permute-done((bf16[56,96,128]{2,1,0:T(8,128)(2,1)}, bf16[56,96,128]{2,1,0:T(8,128)(2,1)}, u32[]{:S(2)}, u32[]{:S(2)}) %collective-permute-start.2) | collective-permute-done | bytes 1376288 | tf_op jit(solution)/shard_map/ppermute | solution.py:270
  247.8 3.2 %copy.44 = bf16[128,56,96]{2,1,0:T(8,128)(2,1)S(1)} copy(bf16[128,56,96]{0,2,1:T(8,128)(2,1)} %bitcast.32) | data formatting | bytes 2752512 | tf_op jit(solution)/shard_map/optimization_barrier | solution.py:276
  251.0 3.2 %convolution_add_fusion = f32[64,112,128]{2,1,0:T(8,128)S(1)} fusion(f32[64,112,128]{2,1,0:T(8,128)} %fusion.14, bf16[64,112,96]{2,1,0:T(8,128)(2,1)S(1)} %bitcast.128, bf16[64,96,128]{2,1,0:T(8,128)(2,1)S(1)} %get-tuple-element.16.table_ref), kind=kOutput, calls=%fused_computation.7 | convolution fusion | flops 177078272 | bytes 10289152 | tf_op jit(solution)/shard_map/mrj,mjn->mrn/dot_general | solution.py:278
  254.2 3.4 %fusion.35 = f32[128,128,56]{1,2,0:T(8,128)S(1)} fusion(f32[128,56,128]{2,1,0:T(8,128)S(1)} %bitcast.121, f32[56,56]{1,0:T(8,128)S(1)} %copy-done), kind=kOutput, calls=%fused_computation.51 | convolution fusion | flops 616562688 | bytes 7352576 | tf_op jit(solution)/shard_map/kl,pmln->pmkn/dot_general | solution.py:60
  257.6 3.6 %fusion.11 = bf16[128,128,56]{1,2,0:T(8,128)(2,1)S(1)} fusion(f32[128,128,56]{1,2,0:T(8,128)S(1)} %fusion.35, f32[56,128]{1,0:T(8,128)S(1)} %multiply_add_fusion, f32[56,56]{1,0:T(8,128)S(1)} %copy-done.19), kind=kOutput, calls=%fused_computation.13 | convolution fusion | flops 618397696 | bytes 5546240 | tf_op jit(solution)/shard_map/lk,pmkn->pmln/dot_general | solution.py:63
  261.2 1.6 shard_map.87
  262.9 1.2 copy-done.6
  264.1 3.9 %copy.47 = bf16[128,56,96]{0,2,1:T(8,128)(2,1)} copy(bf16[128,56,96]{2,1,0:T(8,128)(2,1)} %bitcast.114) | data formatting | bytes 2752512 | tf_op jit(solution)/shard_map/optimization_barrier | solution.py:289
  268.0 1.5 collective-permute-start.3
  269.5 1.6 shard_map.86
  271.1 1.2 copy-done.4
  272.3 3.4 %copy.46 = bf16[128,56,96]{0,2,1:T(8,128)(2,1)S(1)} copy(bf16[128,56,96]{2,1,0:T(8,128)(2,1)} %bitcast.112) | data formatting | bytes 2752512 | tf_op jit(solution)/shard_map/optimization_barrier | solution.py:289
  275.8 23.7 %collective-permute-done.3.refs_1_ = bf16[56,96,128]{2,1,0:T(8,128)(2,1)} collective-permute-done((bf16[56,96,128]{2,1,0:T(8,128)(2,1)}, bf16[56,96,128]{2,1,0:T(8,128)(2,1)}, u32[]{:S(2)}, u32[]{:S(2)}) %collective-permute-start.3) | collective-permute-done | bytes 1376288 | tf_op jit(solution)/shard_map/ppermute | solution.py:270
  299.5 7.1 %shard_map.88 = f32[56,96,384]{2,1,0:T(8,128)} custom-call(bf16[256,384]{1,0:T(8,128)(2,1)S(1)} %copy-done.13, bf16[56,96,128]{2,1,0:T(8,128)(2,1)S(1)} %bitcast.117, bf16[56,96,128]{2,1,0:T(8,128)(2,1)} %collective-permute-done.3.refs_1_), custom_call_target="tpu_custom_call" | custom-call | tf_op jit(solution)/shard_map/pallas_call | solution.py:173
  (61 shorter events, 5.0 us)
Async XLA Ops:
  0.0 53.8 %copy-start = (f32[56,56]{1,0:T(8,128)S(1)}, f32[56,56]{1,0:T(8,128)}, u32[]{:S(2)}) copy-start(f32[56,56]{1,0:T(8,128)} %param.13) | copy-start | bytes 37636
  2.5 11.9 %copy-start.10 = (bf16[384,256]{1,0:T(8,128)(2,1)}, bf16[384,256]{1,0:T(8,128)(2,1)S(1)}, u32[]{:S(2)}) copy-start(bf16[384,256]{1,0:T(8,128)(2,1)S(1)} %pad_maximum_fusion.1.forward_ref) | copy-start | bytes 589828
  3.8 10.6 %copy-start.8 = (bf16[448,448]{1,0:T(8,128)(2,1)}, bf16[448,448]{1,0:T(8,128)(2,1)S(1)}, u32[]{:S(2)}) copy-start(bf16[448,448]{1,0:T(8,128)(2,1)S(1)} %fusion.20.mixer_ref) | copy-start | bytes 1204228
  3.9 3.4 %copy-start.3 = (f32[1,56,96,384]{3,2,1,0:T(8,128)S(1)}, f32[1,56,96,384]{3,2,1,0:T(8,128)}, u32[]{:S(2)}) copy-start(f32[1,56,96,384]{3,2,1,0:T(8,128)} %param.8) | copy-start | bytes 24772612
  14.4 33.3 %collective-permute-start = (bf16[56,96,128]{2,1,0:T(8,128)(2,1)S(1)}, bf16[56,96,128]{2,1,0:T(8,128)(2,1)}, u32[]{:S(2)}, u32[]{:S(2)}) collective-permute-start(bf16[56,96,128]{2,1,0:T(8,128)(2,1)S(1)} %get-tuple-element.10), channel_id=1, source_target_pairs={{0,1},{1,0},{2,3},{3,2},{4,5},{5,4},{6,7},{7,6},{8,9},{9,8},{10,11... | collective-permute-start | bytes 4128776 | tf_op jit(solution)/shard_map/ppermute | solution.py:270
  20.3 3.5 %copy-start.17 = (f32[56]{0:T(128)S(1)}, f32[56]{0:T(128)}, u32[]{:S(2)}) copy-start(f32[56]{0:T(128)} %param.15) | copy-start | bytes 676
  20.3 3.5 %copy-start.15 = (bf16[64,192,128]{2,1,0:T(8,128)(2,1)S(1)}, bf16[64,192,128]{2,1,0:T(8,128)(2,1)}, u32[]{:S(2)}) copy-start(bf16[64,192,128]{2,1,0:T(8,128)(2,1)} %param.12) | copy-start | bytes 9437188
  20.4 3.8 %copy-start.16 = (bf16[128,56,96]{2,1,0:T(8,128)(2,1)S(1)}, bf16[128,56,96]{2,1,0:T(8,128)(2,1)}, u32[]{:S(2)}) copy-start(bf16[128,56,96]{2,1,0:T(8,128)(2,1)} %copy.33) | copy-start | bytes 4128772
  53.9 3.4 %copy-start.18 = (f32[56,56]{1,0:T(8,128)S(1)}, f32[56,56]{1,0:T(8,128)}, u32[]{:S(2)}) copy-start(f32[56,56]{1,0:T(8,128)} %param.14) | copy-start | bytes 37636
  62.0 6.9 %copy-start.20 = (u32[32]{0:T(128)S(1)}, u32[32]{0:T(128)}, u32[]{:S(2)}) copy-start(u32[32]{0:T(128)} %constant.209) | copy-start | bytes 388
  62.0 50.6 %all-to-all-start = ((bf16[16,448,128]{2,1,0:T(8,128)(2,1)}), bf16[16,448,128]{2,1,0:T(8,128)(2,1)S(1)}, u32[]{:S(2)}, u32[]{:S(2)}) async-start(bf16[16,448,128]{2,1,0:T(8,128)(2,1)} %bitcast.129), calls=%async_computation | async-start | bytes 3670016 | tf_op jit(solution)/shard_map/all_to_all | solution.py:224
  164.2 1.2 copy-start.7
  169.2 33.2 %collective-permute-start.1 = (bf16[56,96,128]{2,1,0:T(8,128)(2,1)}, bf16[56,96,128]{2,1,0:T(8,128)(2,1)}, u32[]{:S(2)}, u32[]{:S(2)}) collective-permute-start(bf16[56,96,128]{2,1,0:T(8,128)(2,1)} %bitcast.130), channel_id=1, source_target_pairs={{0,1},{1,0},{2,3},{3,2},{4,5},{5,4},{6,7},{7,6},{8,9},{9,8},{10,11... | collective-permute-start | bytes 4128776 | tf_op jit(solution)/shard_map/ppermute | solution.py:270
  173.4 1.4 copy-start.1
  176.4 1.2 copy-start.5
  177.6 24.8 %copy-start.9 = (bf16[448,448]{1,0:T(8,128)(2,1)S(1)}, bf16[448,448]{1,0:T(8,128)(2,1)}, u32[]{:S(2)}) copy-start(bf16[448,448]{1,0:T(8,128)(2,1)} %copy-done.8) | copy-start | bytes 1204228
  202.4 0.9 copy-start.11
  203.3 0.9 copy-start.12
  214.5 1.1 copy-start.14
  215.5 32.3 %collective-permute-start.2 = (bf16[56,96,128]{2,1,0:T(8,128)(2,1)}, bf16[56,96,128]{2,1,0:T(8,128)(2,1)}, u32[]{:S(2)}, u32[]{:S(2)}) collective-permute-start(bf16[56,96,128]{2,1,0:T(8,128)(2,1)} %get-tuple-element.12), channel_id=1, source_target_pairs={{0,1},{1,0},{2,3},{3,2},{4,5},{5,4},{6,7},{7,6},{8,9},{9,8},{10,11... | collective-permute-start | bytes 4128776 | tf_op jit(solution)/shard_map/ppermute | solution.py:270
  254.2 3.4 %copy-start.19 = (f32[56,56]{1,0:T(8,128)S(1)}, f32[56,56]{1,0:T(8,128)}, u32[]{:S(2)}) copy-start(f32[56,56]{1,0:T(8,128)} %param.14) | copy-start | bytes 37636
  262.9 1.2 copy-start.6
  264.1 5.4 %copy-start.2 = (bf16[64,96,128]{2,1,0:T(8,128)(2,1)S(1)}, bf16[64,96,128]{2,1,0:T(8,128)(2,1)}, u32[]{:S(2)}) copy-start(bf16[64,96,128]{2,1,0:T(8,128)(2,1)} %get-tuple-element.15.table_ref) | copy-start | bytes 4718596
  268.0 31.4 %collective-permute-start.3 = (bf16[56,96,128]{2,1,0:T(8,128)(2,1)}, bf16[56,96,128]{2,1,0:T(8,128)(2,1)}, u32[]{:S(2)}, u32[]{:S(2)}) collective-permute-start(bf16[56,96,128]{2,1,0:T(8,128)(2,1)} %bitcast.131), channel_id=1, source_target_pairs={{0,1},{1,0},{2,3},{3,2},{4,5},{5,4},{6,7},{7,6},{8,9},{9,8},{10,11... | collective-permute-start | bytes 4128776 | tf_op jit(solution)/shard_map/ppermute | solution.py:270
  271.1 1.2 copy-start.4
  272.3 27.1 %copy-start.13 = (bf16[256,384]{1,0:T(8,128)(2,1)S(1)}, bf16[256,384]{1,0:T(8,128)(2,1)}, u32[]{:S(2)}) copy-start(bf16[256,384]{1,0:T(8,128)(2,1)} %pad_maximum_fusion.backward_ref) | copy-start | bytes 589828
